TPU v7x, 128 devices: a whole 4x4x4 slice. The times are simulated.
128 devices in a mesh: ctx: 32 (over x, z, y_hi), fsdp: 4 (over y_lo, core).
Axes of the slice: x: 4, y: 4 (y_hi: 2, y_lo: 2; y = y_hi * 2 + y_lo), z: 4, core: 2. Of those that a mesh axis runs over, the one named last changes fastest.
Arguments:
- block_input: bfloat16 [4, 4096, 1024], P('fsdp', 'ctx'), may hold values from -6 to 6
- routes: int32 [4, 4096, 8], P('fsdp', 'ctx'), may hold values from 0 to 31, all different within a row; in each aligned block of 128 rows (0 to 127, 128 to 255, ..., all dimensions but the last counted through in order) at most 48 rows name the same one
- block_pairs: int32 [32], replicated, may hold values from 0 to 31, each once
- norm1_gain: bfloat16 [1024], P('fsdp'), may hold values from 0.5 to 1.5
- w_query: bfloat16 [1024, 1024], P('fsdp'), may hold values from -0.75 to 0.75
- w_key: bfloat16 [1024, 512], P('fsdp'), may hold values from -0.75 to 0.75
- w_value: bfloat16 [1024, 512], P('fsdp'), may hold values from -0.1875 to 0.1875
- w_out: bfloat16 [1024, 1024], P('fsdp'), may hold values from -4 to 4
- norm2_gain: bfloat16 [1024], P('fsdp'), may hold values from 0.5 to 1.5
- w_router: bfloat16 [1024, 32], P('fsdp'), may hold values from -0.09375 to 0.09375
- w_gate: bfloat16 [32, 1024, 512], P('ctx', 'fsdp'), may hold values from -0.1875 to 0.1875
- w_up: bfloat16 [32, 1024, 512], P('ctx', 'fsdp'), may hold values from -0.1875 to 0.1875
- w_down: bfloat16 [32, 512, 1024], P('ctx', 'fsdp'), may hold values from -4 to 4
- cotangent: bfloat16 [4, 4096, 1024], P('fsdp', 'ctx'), may hold values from -6 to 6
Outputs:
- block_output: bfloat16 [4, 4096, 1024], P('fsdp', 'ctx')
- input_grad: float32 [4, 4096, 1024], P('fsdp', 'ctx')
- norm1_gain_grad: float32 [1024], P('fsdp')
- w_query_grad: float32 [1024, 1024], P('fsdp')
- w_key_grad: float32 [1024, 512], P('fsdp')
- w_value_grad: float32 [1024, 512], P('fsdp')
- w_out_grad: float32 [1024, 1024], P('fsdp')
- norm2_gain_grad: float32 [1024], P('fsdp')
- w_router_grad: float32 [1024, 32], P('fsdp')
- w_gate_grad: float32 [32, 1024, 512], P('ctx', 'fsdp')
- w_up_grad: float32 [32, 1024, 512], P('ctx', 'fsdp')
- w_down_grad: float32 [32, 512, 1024], P('ctx', 'fsdp')
Inputs may be any that keep to these rules, and one draw needn't show every extreme that they name: `routes`: each row names 8 different experts; among the 128 rows of one device no expert is named more than 48 times, a bound that some block reaches. `block_pairs`: each number appears once. Index c of ctx holds, in this order, the blocks of half of 128 tokens numbered block_pairs[c] and 63 - block_pairs[c].
All inputs are finite; a program needn't handle non-finite values.
Results may differ from a plain program's by a relative error of at most 0.035.
Values may be sent and summed in bfloat16 or wider, within the bound.
No kernel may reach another device: no remote copies, remote signals or barrier semaphores. Data moves between devices by JAX's collectives and lax.ppermute only.
A program may use at most 128 MiB of HBM per device.

v0:
```python
import math

import jax
import jax.numpy as jnp
from jax import lax
from jax.sharding import PartitionSpec as P

HEADS = 16
KV_HEADS = 8
HEAD_DIM = 64
EXPERTS = 32
TOP = 8
CAP = 48


epsilon = 1e-06
attn_scale = 0.015625
residual_scale = 0.22
masked_value = -1e30


def product(left, right):
    return jnp.dot(left, right, preferred_element_type=jnp.float32)


def contract(form, left, right):
    return jnp.einsum(form, left, right, preferred_element_type=jnp.float32)


def positions_of(rows, block_pairs, tok_rows, ctx_count):
    device = rows // tok_rows
    local = rows % tok_rows
    half_rows = tok_rows // 2
    first = jnp.sum(
        jnp.where(
            device[:, None] == jnp.arange(ctx_count, dtype=jnp.int32)[None, :],
            block_pairs[None, :],
            0,
        ),
        axis=1,
    )
    number = jnp.where(local < half_rows, first, 2 * ctx_count - 1 - first)
    return number * half_rows + local % half_rows


def rope_tables(positions, head_width):
    freqs = jnp.power(10000.0, -jnp.arange(0, head_width, 2, dtype=jnp.float32) / head_width)
    angles = positions.astype(jnp.float32)[:, None] * freqs[None, :]
    angles = jnp.concatenate([angles, angles], axis=-1)
    return (jnp.cos(angles), jnp.sin(angles))


def rotate(values, cosine, sine):
    middle = values.shape[-1] // 2
    turned = jnp.concatenate([-values[..., middle:], values[..., :middle]], axis=-1)
    return values * cosine[:, None, :] + turned * sine[:, None, :]


def rotate_back(grads, cosine, sine):
    middle = grads.shape[-1] // 2
    scaled = grads * sine[:, None, :]
    turned = jnp.concatenate([scaled[..., middle:], -scaled[..., :middle]], axis=-1)
    return grads * cosine[:, None, :] + turned


def to_groups(rows_heads, row_count):
    group_share = HEADS // KV_HEADS
    shaped = rows_heads.reshape(row_count, KV_HEADS, group_share, HEAD_DIM)
    return shaped.transpose(1, 2, 0, 3).reshape(KV_HEADS, group_share * row_count, HEAD_DIM)


def from_groups(grouped, row_count):
    group_share = HEADS // KV_HEADS
    shaped = grouped.reshape(KV_HEADS, group_share, row_count, HEAD_DIM)
    return shaped.transpose(2, 0, 1, 3).reshape(row_count, HEADS * HEAD_DIM)


def scores_of(query_g, query_pos_g, key_part, pos_part):
    key_count = key_part.shape[0]
    key_heads = key_part.reshape(key_count, KV_HEADS, HEAD_DIM)
    raw_scores = contract("hqd,khd->hqk", query_g, key_heads) * attn_scale
    return jnp.where(
        pos_part[None, None, :] <= query_pos_g[None, :, None], raw_scores, masked_value
    )


def block_grads(key_part, value_part, pos_part, query_g, query_pos_g, grad_g, log_total, row_dots):
    key_count = key_part.shape[0]
    scores = scores_of(query_g, query_pos_g, key_part, pos_part)
    probs_f = jnp.exp(scores - log_total[..., None])
    prob_grad = contract("hqd,khd->hqk", grad_g, value_part.reshape(key_count, KV_HEADS, HEAD_DIM))
    score_grad = (probs_f * (prob_grad - row_dots[..., None])).astype(jnp.bfloat16)
    return (probs_f.astype(jnp.bfloat16), score_grad)


def norm_back(values, inv_rms, gain, grad):
    weighted = grad * gain
    gain_grad = jnp.sum(grad * values * inv_rms, axis=0)
    inner_mean = jnp.mean(weighted * values, axis=-1, keepdims=True)
    return (weighted * inv_rms - values * inv_rms * inv_rms * inv_rms * inner_mean, gain_grad)


def on_device(
    block_input,
    routes,
    block_pairs,
    norm1_gain,
    w_query,
    w_key,
    w_value,
    w_out,
    norm2_gain,
    w_router,
    w_gate,
    w_up,
    w_down,
    cotangent,
):
    tok_rows = block_input.shape[1]
    model_width = block_input.shape[2]
    ctx_count = lax.axis_size("ctx")
    group_share = HEADS // KV_HEADS
    seq_rows = tok_rows * ctx_count
    grouped_rows = group_share * tok_rows
    span_rows = math.gcd(512, seq_rows)
    span_count = seq_rows // span_rows
    local_experts = EXPERTS // ctx_count
    inputs = block_input[0].astype(jnp.float32)
    gain_one, query_w, key_w, value_w, out_w, gain_two, router_w = (
        lax.all_gather(norm1_gain, "fsdp", axis=0, tiled=True),
        lax.all_gather(w_query, "fsdp", axis=0, tiled=True),
        lax.all_gather(w_key, "fsdp", axis=0, tiled=True),
        lax.all_gather(w_value, "fsdp", axis=0, tiled=True),
        lax.all_gather(w_out, "fsdp", axis=0, tiled=True),
        lax.all_gather(norm2_gain, "fsdp", axis=0, tiled=True),
        lax.all_gather(w_router, "fsdp", axis=0, tiled=True),
    )
    gate_w, up_w, down_w = (
        lax.all_gather(w_gate, "fsdp", axis=1, tiled=True),
        lax.all_gather(w_up, "fsdp", axis=1, tiled=True),
        lax.all_gather(w_down, "fsdp", axis=1, tiled=True),
    )
    gain_one = gain_one.astype(jnp.float32)
    gain_two = gain_two.astype(jnp.float32)
    own_index = lax.axis_index("ctx")
    query_pos = positions_of(
        jnp.arange(tok_rows, dtype=jnp.int32) + own_index * tok_rows,
        block_pairs,
        tok_rows,
        ctx_count,
    )
    key_pos = positions_of(jnp.arange(seq_rows, dtype=jnp.int32), block_pairs, tok_rows, ctx_count)
    query_pos_g = jnp.tile(query_pos, group_share)
    cosine, sine = rope_tables(query_pos, HEAD_DIM)
    inv_rms1 = lax.rsqrt(jnp.mean(inputs * inputs, axis=-1, keepdims=True) + epsilon)
    normed1 = (inputs * inv_rms1 * gain_one).astype(jnp.bfloat16)
    query_raw = product(normed1, query_w).reshape(tok_rows, HEADS, HEAD_DIM)
    key_raw = product(normed1, key_w).reshape(tok_rows, KV_HEADS, HEAD_DIM)
    value_rows = product(normed1, value_w).astype(jnp.bfloat16)
    query_rot = (
        rotate(query_raw, cosine, sine).astype(jnp.bfloat16).reshape(tok_rows, HEADS * HEAD_DIM)
    )
    key_rot = (
        rotate(key_raw, cosine, sine).astype(jnp.bfloat16).reshape(tok_rows, KV_HEADS * HEAD_DIM)
    )
    key_all, value_all = (
        lax.all_gather(key_rot, "ctx", axis=0, tiled=True),
        lax.all_gather(value_rows, "ctx", axis=0, tiled=True),
    )
    query_g = to_groups(query_rot, tok_rows)

    def key_span(counter):
        offset = counter * span_rows
        return (
            lax.dynamic_slice_in_dim(key_all, offset, span_rows, 0),
            lax.dynamic_slice_in_dim(value_all, offset, span_rows, 0),
            lax.dynamic_slice_in_dim(key_pos, offset, span_rows, 0),
        )

    def max_pass(counter, running):
        running_max, running_sum = running
        key_part, value_part, pos_part = key_span(counter)
        scores = scores_of(query_g, query_pos_g, key_part, pos_part)
        new_max = jnp.maximum(running_max, jnp.max(scores, axis=-1))
        running_sum = running_sum * jnp.exp(running_max - new_max) + jnp.sum(
            jnp.exp(scores - new_max[..., None]), axis=-1
        )
        return (new_max, running_sum)

    start_max = jnp.full((KV_HEADS, grouped_rows), masked_value, jnp.float32)
    start_sum = jnp.zeros((KV_HEADS, grouped_rows), jnp.float32)
    running_max, running_sum = lax.fori_loop(0, span_count, max_pass, (start_max, start_sum))
    log_total = running_max + jnp.log(running_sum)

    def out_pass(counter, accum_out):
        key_part, value_part, pos_part = key_span(counter)
        scores = scores_of(query_g, query_pos_g, key_part, pos_part)
        attn_probs = jnp.exp(scores - log_total[..., None]).astype(jnp.bfloat16)
        return accum_out + contract(
            "hqk,khd->hqd", attn_probs, value_part.reshape(span_rows, KV_HEADS, HEAD_DIM)
        )

    attn_g = lax.fori_loop(
        0, span_count, out_pass, jnp.zeros((KV_HEADS, grouped_rows, HEAD_DIM), jnp.float32)
    )
    attn_rows = from_groups(attn_g, tok_rows).astype(jnp.bfloat16)
    hidden = inputs + residual_scale * product(attn_rows, out_w)
    inv_rms2 = lax.rsqrt(jnp.mean(hidden * hidden, axis=-1, keepdims=True) + epsilon)
    normed2 = (hidden * inv_rms2 * gain_two).astype(jnp.bfloat16)
    logits = product(normed2, router_w)
    chosen = routes[0]
    picked = (chosen[:, :, None] == jnp.arange(EXPERTS, dtype=jnp.int32)[None, None, :]).astype(
        jnp.float32
    )
    selected = jnp.sum(picked * logits[:, None, :], axis=-1)
    gate_probs = jax.nn.softmax(selected, axis=-1)
    flat_routes = chosen.reshape(-1)
    onehot = (flat_routes[:, None] == jnp.arange(EXPERTS, dtype=jnp.int32)[None, :]).astype(
        jnp.int32
    )
    slot_rank = jnp.sum((jnp.cumsum(onehot, axis=0) - onehot) * onehot, axis=1)
    slot_index = flat_routes * CAP + slot_rank
    route_rows = jnp.repeat(normed2, TOP, axis=0)
    outgoing = (
        jnp.zeros((EXPERTS * CAP, model_width), jnp.bfloat16)
        .at[slot_index]
        .set(route_rows)
        .reshape(EXPERTS, CAP, model_width)
    )
    arrived = lax.all_to_all(outgoing, "ctx", split_axis=0, concat_axis=0, tiled=True).reshape(
        ctx_count, local_experts, CAP, model_width
    )
    gate_pre = contract("secd,edf->secf", arrived, gate_w)
    up_pre = contract("secd,edf->secf", arrived, up_w)
    sigmoid_a = jax.nn.sigmoid(gate_pre)
    swish_act = gate_pre * sigmoid_a
    inner_act = (swish_act * up_pre).astype(jnp.bfloat16)
    expert_out = contract("secf,efd->secd", inner_act, down_w).astype(jnp.bfloat16)
    returned = lax.all_to_all(
        expert_out.reshape(EXPERTS, CAP, model_width),
        "ctx",
        split_axis=0,
        concat_axis=0,
        tiled=True,
    )
    per_route = (
        returned.reshape(EXPERTS * CAP, model_width)[slot_index]
        .reshape(tok_rows, TOP, model_width)
        .astype(jnp.float32)
    )
    mixture = jnp.sum(gate_probs[..., None] * per_route, axis=1)
    output = hidden + residual_scale * mixture
    upstream = cotangent[0].astype(jnp.float32)
    mix_grad = residual_scale * upstream
    gate_grad = jnp.sum(mix_grad[:, None, :] * per_route, axis=-1)
    route_grad = (
        (gate_probs[..., None] * mix_grad[:, None, :])
        .astype(jnp.bfloat16)
        .reshape(tok_rows * TOP, model_width)
    )
    back_send = (
        jnp.zeros((EXPERTS * CAP, model_width), jnp.bfloat16)
        .at[slot_index]
        .set(route_grad)
        .reshape(EXPERTS, CAP, model_width)
    )
    back_arrived = lax.all_to_all(
        back_send, "ctx", split_axis=0, concat_axis=0, tiled=True
    ).reshape(ctx_count, local_experts, CAP, model_width)
    grad_down = contract("secf,secd->efd", inner_act, back_arrived)
    inner_grad = contract("secd,efd->secf", back_arrived, down_w)
    gate_pre_grad = (inner_grad * up_pre * sigmoid_a * (1.0 + gate_pre * (1.0 - sigmoid_a))).astype(
        jnp.bfloat16
    )
    up_pre_grad = (inner_grad * swish_act).astype(jnp.bfloat16)
    grad_gate = contract("secd,secf->edf", arrived, gate_pre_grad)
    grad_up = contract("secd,secf->edf", arrived, up_pre_grad)
    expert_in_grad = (
        contract("secf,edf->secd", gate_pre_grad, gate_w)
        + contract("secf,edf->secd", up_pre_grad, up_w)
    ).astype(jnp.bfloat16)
    back_returned = lax.all_to_all(
        expert_in_grad.reshape(EXPERTS, CAP, model_width),
        "ctx",
        split_axis=0,
        concat_axis=0,
        tiled=True,
    )
    normed2_grad = jnp.sum(
        back_returned.reshape(EXPERTS * CAP, model_width)[slot_index]
        .reshape(tok_rows, TOP, model_width)
        .astype(jnp.float32),
        axis=1,
    )
    mean_grad = jnp.sum(gate_probs * gate_grad, axis=-1, keepdims=True)
    select_grad = gate_probs * (gate_grad - mean_grad)
    logit_grad = jnp.sum(picked * select_grad[..., None], axis=1).astype(jnp.bfloat16)
    grad_router = product(normed2.T, logit_grad)
    normed2_grad = normed2_grad + product(logit_grad, router_w.T)
    hidden_part, gain_two_grad = norm_back(hidden, inv_rms2, gain_two, normed2_grad)
    hidden_grad = upstream + hidden_part
    branch_grad = (residual_scale * hidden_grad).astype(jnp.bfloat16)
    grad_out = product(attn_rows.T, branch_grad)
    attn_grad = product(branch_grad, out_w.T).astype(jnp.bfloat16)
    attn_grad_g = to_groups(attn_grad, tok_rows)

    def dot_pass(counter, row_dots):
        key_part, value_part, pos_part = key_span(counter)
        scores = scores_of(query_g, query_pos_g, key_part, pos_part)
        probs_f = jnp.exp(scores - log_total[..., None])
        prob_grad = contract(
            "hqd,khd->hqk", attn_grad_g, value_part.reshape(span_rows, KV_HEADS, HEAD_DIM)
        )
        return row_dots + jnp.sum(probs_f * prob_grad, axis=-1)

    row_dots = lax.fori_loop(
        0, span_count, dot_pass, jnp.zeros((KV_HEADS, grouped_rows), jnp.float32)
    )
    zero_query = jnp.zeros((KV_HEADS, grouped_rows, HEAD_DIM), jnp.float32)

    def grad_pass(counter, running):
        query_acc, key_acc, value_acc = running
        key_part, value_part, pos_part = key_span(counter)
        probs_b, score_grad = block_grads(
            key_part, value_part, pos_part, query_g, query_pos_g, attn_grad_g, log_total, row_dots
        )
        query_acc = query_acc + contract(
            "hqk,khd->hqd", score_grad, key_part.reshape(span_rows, KV_HEADS, HEAD_DIM)
        )
        key_new = (
            contract("hqk,hqd->khd", score_grad, query_g).reshape(span_rows, KV_HEADS * HEAD_DIM)
            * attn_scale
        )
        value_new = contract("hqk,hqd->khd", probs_b, attn_grad_g).reshape(
            span_rows, KV_HEADS * HEAD_DIM
        )
        offset = counter * span_rows
        key_acc = lax.dynamic_update_slice_in_dim(key_acc, key_new, offset, 0)
        value_acc = lax.dynamic_update_slice_in_dim(value_acc, value_new, offset, 0)
        return (query_acc, key_acc, value_acc)

    zero_keys = jnp.zeros((seq_rows, KV_HEADS * HEAD_DIM), jnp.float32)
    query_acc, key_acc, value_acc = lax.fori_loop(
        0, span_count, grad_pass, (zero_query, zero_keys, zero_keys)
    )
    key_sum, value_sum = (
        lax.psum_scatter(
            key_acc.astype(jnp.bfloat16), "ctx", scatter_dimension=0, tiled=True
        ).astype(jnp.float32),
        lax.psum_scatter(
            value_acc.astype(jnp.bfloat16), "ctx", scatter_dimension=0, tiled=True
        ).astype(jnp.float32),
    )
    key_grad = (
        rotate_back(key_sum.reshape(tok_rows, KV_HEADS, HEAD_DIM), cosine, sine)
        .reshape(tok_rows, KV_HEADS * HEAD_DIM)
        .astype(jnp.bfloat16)
    )
    value_grad = value_sum.astype(jnp.bfloat16)
    query_part_rows = (from_groups(query_acc, tok_rows) * attn_scale).reshape(
        tok_rows, HEADS, HEAD_DIM
    )
    query_grad = (
        rotate_back(query_part_rows, cosine, sine)
        .reshape(tok_rows, HEADS * HEAD_DIM)
        .astype(jnp.bfloat16)
    )
    grad_query = product(normed1.T, query_grad)
    grad_key = product(normed1.T, key_grad)
    grad_value = product(normed1.T, value_grad)
    normed1_grad = (
        product(query_grad, query_w.T) + product(key_grad, key_w.T) + product(value_grad, value_w.T)
    )
    input_part, gain_one_grad = norm_back(inputs, inv_rms1, gain_one, normed1_grad)
    input_grad = hidden_grad + input_part
    dense_sums = (
        lax.psum_scatter(
            gain_one_grad.astype(jnp.bfloat16), "fsdp", scatter_dimension=0, tiled=True
        ).astype(jnp.float32),
        lax.psum_scatter(
            grad_query.astype(jnp.bfloat16), "fsdp", scatter_dimension=0, tiled=True
        ).astype(jnp.float32),
        lax.psum_scatter(
            grad_key.astype(jnp.bfloat16), "fsdp", scatter_dimension=0, tiled=True
        ).astype(jnp.float32),
        lax.psum_scatter(
            grad_value.astype(jnp.bfloat16), "fsdp", scatter_dimension=0, tiled=True
        ).astype(jnp.float32),
        lax.psum_scatter(
            grad_out.astype(jnp.bfloat16), "fsdp", scatter_dimension=0, tiled=True
        ).astype(jnp.float32),
        lax.psum_scatter(
            gain_two_grad.astype(jnp.bfloat16), "fsdp", scatter_dimension=0, tiled=True
        ).astype(jnp.float32),
        lax.psum_scatter(
            grad_router.astype(jnp.bfloat16), "fsdp", scatter_dimension=0, tiled=True
        ).astype(jnp.float32),
    )
    dense_sums = (
        lax.psum(dense_sums[0].astype(jnp.bfloat16), "ctx").astype(jnp.float32),
        lax.psum(dense_sums[1].astype(jnp.bfloat16), "ctx").astype(jnp.float32),
        lax.psum(dense_sums[2].astype(jnp.bfloat16), "ctx").astype(jnp.float32),
        lax.psum(dense_sums[3].astype(jnp.bfloat16), "ctx").astype(jnp.float32),
        lax.psum(dense_sums[4].astype(jnp.bfloat16), "ctx").astype(jnp.float32),
        lax.psum(dense_sums[5].astype(jnp.bfloat16), "ctx").astype(jnp.float32),
        lax.psum(dense_sums[6].astype(jnp.bfloat16), "ctx").astype(jnp.float32),
    )
    expert_sums = (
        lax.psum_scatter(
            grad_gate.astype(jnp.bfloat16), "fsdp", scatter_dimension=1, tiled=True
        ).astype(jnp.float32),
        lax.psum_scatter(
            grad_up.astype(jnp.bfloat16), "fsdp", scatter_dimension=1, tiled=True
        ).astype(jnp.float32),
        lax.psum_scatter(
            grad_down.astype(jnp.bfloat16), "fsdp", scatter_dimension=1, tiled=True
        ).astype(jnp.float32),
    )
    return (
        output.astype(jnp.bfloat16)[None],
        input_grad[None],
        dense_sums[0],
        dense_sums[1],
        dense_sums[2],
        dense_sums[3],
        dense_sums[4],
        dense_sums[5],
        dense_sums[6],
        expert_sums[0],
        expert_sums[1],
        expert_sums[2],
    )


def solution(mesh):
    return jax.shard_map(
        on_device,
        mesh=mesh,
        in_specs=(
            P("fsdp", "ctx", None),
            P("fsdp", "ctx", None),
            P(),
            P("fsdp"),
            P("fsdp", None),
            P("fsdp", None),
            P("fsdp", None),
            P("fsdp", None),
            P("fsdp"),
            P("fsdp", None),
            P("ctx", "fsdp", None),
            P("ctx", "fsdp", None),
            P("ctx", "fsdp", None),
            P("fsdp", "ctx", None),
        ),
        out_specs=(
            P("fsdp", "ctx", None),
            P("fsdp", "ctx", None),
            P("fsdp"),
            P("fsdp", None),
            P("fsdp", None),
            P("fsdp", None),
            P("fsdp", None),
            P("fsdp"),
            P("fsdp", None),
            P("ctx", "fsdp", None),
            P("ctx", "fsdp", None),
            P("ctx", "fsdp", None),
        ),
        check_vma=False,
    )
```

profile of v0, /device:TPU:0, one launch (start us, length us, event | category | flops | bytes accessed | tf_op | source)
XLA Modules:
  0.0 1643.1 jit_solution(15479961185872249664)
XLA Ops:
  10.1 5.1 all-gather
  17.9 15.0 all-gather.12.cloned.1.call-done
  35.7 20.5 %all-gather.18.cloned.1.call-done = bf16[1024,512]{1,0:T(8,128)(2,1)} async-done(((bf16[256,512]{1,0:T(8,128)(2,1)}), bf16[1024,512]{1,0:T(8,128)(2,1)}) %all-gather.18.cloned.1.call-update) | async-done | bytes 1048592 | tf_op jit(solution)/shard_map/all_gather | solution.py:133
  56.2 2.2 convolution_convert_fusion.6
  59.4 5.1 all-gather.1
  64.9 9.0 reduce-window.6
  74.4 13.3 all-gather.16.cloned.1.call-done
  87.8 2.9 copy.175
  91.6 82.2 %all-gather.14.cloned.1.call-done = bf16[4096,512]{0,1:T(8,128)(2,1)} async-done(((bf16[128,512]{0,1:T(8,128)(2,1)}), bf16[4096,512]{0,1:T(8,128)(2,1)}) %all-gather.14.cloned.1.call-update) | async-done | bytes 4194320 | tf_op jit(solution)/shard_map/all_gather | solution.py:167
  173.8 25.1 %while.62 = (s32[]{:T(128)}, f32[8,256]{1,0:T(8,128)S(1)}, f32[8,256]{1,0:T(8,128)S(1)}, s32[4096]{0:T(1024)S(1)}, bf16[4096,512]{0,1:T(8,128)(2,1)}, /*index=5*...) while((s32[]{:T(128)}, f32[8,256]{1,0:T(8,128)S(1)}, ...), condition=%wide.region_6.7_spmd.clone, body=%wide.region_3.6_spmd.clone.sunk | while | flops 141699072 | bytes 10732214 | solution.py:192
  198.9 58.2 %all-gather.20.cloned.1.call-done = bf16[4096,512]{1,0:T(8,128)(2,1)} async-done(((bf16[128,512]{1,0:T(8,128)(2,1)}), bf16[4096,512]{1,0:T(8,128)(2,1)}) %all-gather.20.cloned.1.call-update) | async-done | bytes 4194320 | tf_op jit(solution)/shard_map/all_gather | solution.py:168
  257.1 6.5 copy.177
  263.5 25.3 %while.63 = (s32[]{:T(128)}, f32[8,256,64]{1,2,0:T(8,128)S(1)}, s32[4096]{0:T(1024)S(1)}, bf16[4096,512]{0,1:T(8,128)(2,1)}, bf16[8,256,64]{1,2,0:T(8,128)(2,1)S...) while((s32[]{:T(128)}, f32[8,256,64]{1,2,0:T(8,128)S(1)}, ...), condition=%wide.region_8.9_spmd.clone, body=%wide.region_7.8_spmd.clone.sunk | while | flops 273022976 | bytes 4735677 | solution.py:203
  289.1 2.2 multiply_reduce_fusion.2
  292.2 7.9 scatter_custom_fusion
  300.3 5.8 all-to-all-start
  306.8 42.1 %all_gather.44 = bf16[1024,32]{0,1:T(8,128)(2,1)S(1)} all-gather(bf16[256,32]{0,1:T(8,128)(2,1)S(1)} %copy-done.38), channel_id=1, replica_groups=mesh['ctx'=32,'fsdp'=4] {'fsdp'}, dimensions={0}, use_global_device_ids=true | all-gather | bytes 81920 | tf_op jit(solution)/shard_map/all_gather | solution.py:136
  350.0 7.8 scatter_custom_fusion.1
  357.8 16.1 all-to-all-start.2
  375.4 5.7 fusion.67
  381.1 37.7 %all-gather.28.cloned.1.call-done = bf16[1,512,1024]{2,1,0:T(8,128)(2,1)} async-done(((bf16[1,128,1024]{2,1,0:T(8,128)(2,1)}), bf16[1,512,1024]{2,1,0:T(8,128)(2,1)}) %all-gather.28.cloned.1.call-update) | async-done | bytes 1048592 | tf_op jit(solution)/shard_map/all_gather | solution.py:141
  419.1 5.7 fusion.63
  424.8 19.1 %all-gather.24.cloned.1.call-done = bf16[1,1024,512]{2,1,0:T(8,128)(2,1)} async-done(((bf16[1,256,512]{2,1,0:T(8,128)(2,1)}), bf16[1,1024,512]{2,1,0:T(8,128)(2,1)}) %all-gather.24.cloned.1.call-update) | async-done | bytes 1048592 | tf_op jit(solution)/shard_map/all_gather | solution.py:139
  443.9 9.1 fusion.51
  453.0 3.5 convolution_convert_fusion
  456.5 9.4 all-to-all-start.1
  465.9 3.7 fusion.53
  469.7 3.5 add_convert_fusion
  473.2 34.5 %all-to-all-done.1 = bf16[32,48,1024]{2,1,0:T(8,128)(2,1)S(1)} async-done(((bf16[32,48,1024]{2,1,0:T(8,128)(2,1)}), bf16[32,48,1024]{2,1,0:T(8,128)(2,1)S(1)}, u32[]{:S(2)}, u32[]{:S(2)}) %all-to-all-start.1) | async-done | bytes 3145760 | tf_op jit(solution)/shard_map/all_to_all | solution.py:239
  509.4 8.2 all-to-all-start.3
  518.6 8.3 gather_fusion
  526.9 4.2 fusion.33
  534.0 25.0 %all-to-all-done.3 = bf16[32,48,1024]{2,1,0:T(8,128)(2,1)S(1)} async-done(((bf16[32,48,1024]{2,1,0:T(8,128)(2,1)}), bf16[32,48,1024]{2,1,0:T(8,128)(2,1)S(1)}, u32[]{:S(2)}, u32[]{:S(2)}) %all-to-all-start.3) | async-done | bytes 3145760 | tf_op jit(solution)/shard_map/all_to_all | solution.py:282
  559.0 5.7 gather_fusion.1
  564.8 3.2 convert_reduce_fusion
  568.0 2.0 multiply_reduce_fusion
  572.0 35.2 %while.64 = (s32[]{:T(128)}, f32[8,256]{1,0:T(8,128)S(1)}, s32[4096]{0:T(1024)}, bf16[4096,512]{0,1:T(8,128)(2,1)}, bf16[8,256,64]{1,2,0:T(8,128)(2,1)S(1)}, /*i...) while((s32[]{:T(128)}, f32[8,256]{1,0:T(8,128)S(1)}, ...), condition=%wide.region_26.27_spmd.clone, body=%wide.region_24.26_spmd.clone.sunk | while | flops 273811456 | bytes 12370629 | solution.py:316
  607.2 2.4 broadcast_in_dim.204.clone
  609.6 2.5 broadcast_in_dim.204
  612.1 71.3 %while.65 = (s32[]{:T(128)}, f32[8,256,64]{1,2,0:T(8,128)S(1)}, bf16[4096,512]{0,1:T(8,128)(2,1)}, bf16[4096,512]{0,1:T(8,128)(2,1)}, s32[4096]{0:T(1024)}, /*in...) while((s32[]{:T(128)}, f32[8,256,64]{1,2,0:T(8,128)S(1)}, ...), condition=%wide.region_28.29_spmd.clone, body=%wide.region_27.28_spmd.clone.sunk | while | flops 682491904 | bytes 28213988 | solution.py:343
  683.4 6.5 copy.199
  690.0 6.5 copy.197
  696.6 5.3 fusion.61
  701.9 4.7 fusion.60
  706.7 5.2 fusion.57
  712.0 2.1 convolution_convert_fusion.1
  715.7 2.2 convolution_convert_fusion.2
  718.0 165.9 %reduce-scatter.33.cloned.1.call-done = bf16[128,512]{1,0:T(8,128)(2,1)} async-done(((bf16[4096,512]{1,0:T(8,128)(2,1)}), bf16[128,512]{1,0:T(8,128)(2,1)}) %reduce-scatter.33.cloned.1.call-update) | async-done | bytes 131088
  883.8 2.4 convolution_convert_fusion.3
  886.3 187.4 %reduce-scatter.31.cloned.1.call-done = bf16[128,512]{1,0:T(8,128)(2,1)} async-done(((bf16[4096,512]{1,0:T(8,128)(2,1)}), bf16[128,512]{1,0:T(8,128)(2,1)}) %reduce-scatter.31.cloned.1.call-update) | async-done | bytes 131088
  1079.0 11.5 reduce-scatter.29.cloned.1.call-done
  1092.3 22.0 %reduce-scatter.27.cloned.1.call-done = bf16[1,256,512]{2,1,0:T(8,128)(2,1)} async-done(((bf16[1,1024,512]{2,1,0:T(8,128)(2,1)}), bf16[1,256,512]{2,1,0:T(8,128)(2,1)}) %reduce-scatter.27.cloned.1.call-update) | async-done | bytes 262160 | tf_op jit(solution)/shard_map/reduce_scatter | solution.py:412
  1114.3 1.8 convert_element_type.322
  1116.1 21.8 %reduce-scatter.25.cloned.1.call-done = bf16[1,256,512]{2,1,0:T(8,128)(2,1)} async-done(((bf16[1,1024,512]{2,1,0:T(8,128)(2,1)}), bf16[1,256,512]{2,1,0:T(8,128)(2,1)}) %reduce-scatter.25.cloned.1.call-update) | async-done | bytes 262160 | tf_op jit(solution)/shard_map/reduce_scatter | solution.py:409
  1137.8 1.8 convert_element_type.319
  1139.6 30.0 %reduce-scatter.21.cloned.1.call-done = bf16[256,1024]{1,0:T(8,128)(2,1)} async-done(((bf16[1024,1024]{1,0:T(8,128)(2,1)}), bf16[256,1024]{1,0:T(8,128)(2,1)}) %reduce-scatter.21.cloned.1.call-update) | async-done | bytes 524304 | tf_op jit(solution)/shard_map/reduce_scatter | solution.py:389
  1169.7 31.4 %reduce-scatter.15.cloned.1.call-done = bf16[256,1024]{1,0:T(8,128)(2,1)} async-done(((bf16[1024,1024]{1,0:T(8,128)(2,1)}), bf16[256,1024]{1,0:T(8,128)(2,1)}) %reduce-scatter.15.cloned.1.call-update) | async-done | bytes 524304 | tf_op jit(solution)/shard_map/reduce_scatter | solution.py:380
  1201.1 24.1 %reduce-scatter.19.cloned.1.call-done = bf16[256,512]{1,0:T(8,128)(2,1)} async-done(((bf16[1024,512]{1,0:T(8,128)(2,1)}), bf16[256,512]{1,0:T(8,128)(2,1)}) %reduce-scatter.19.cloned.1.call-update) | async-done | bytes 262160 | tf_op jit(solution)/shard_map/reduce_scatter | solution.py:386
  1225.2 24.0 %reduce-scatter.17.cloned.1.call-done = bf16[256,512]{1,0:T(8,128)(2,1)} async-done(((bf16[1024,512]{1,0:T(8,128)(2,1)}), bf16[256,512]{1,0:T(8,128)(2,1)}) %reduce-scatter.17.cloned.1.call-update) | async-done | bytes 262160 | tf_op jit(solution)/shard_map/reduce_scatter | solution.py:383
  1252.6 6.3 all-reduce.4
  1259.1 11.2 reduce-scatter.23.cloned.1.call-done
  1270.3 183.4 %all-reduce.2 = (bf16[256]{0:T(256)(128)(2,1)S(1)}, bf16[256]{0:T(256)(128)(2,1)S(1)}, bf16[256,32]{0,1:T(8,128)(2,1)S(1)}) all-reduce(bf16[256]{0:T(256)(128)(2,1)S(1)} %dynamic-slice.1, bf16[256]{0:T(256)(128)(2,1)S(1)} %dynamic-slice.3, ...), channel_id=1, replica_groups=mesh['ctx'=32,'fsdp'=4] {'ctx'}, use_global_device_ids=true, to_apply=%region_34.35 | all-reduce | flops 8704 | bytes 34816 | tf_op jit(solution)/shard_map/psum | solution.py:400
  1456.5 172.4 %all-reduce.7.cloned.1.call-done = (bf16[256,1024]{1,0:T(8,128)(2,1)}, bf16[256,512]{1,0:T(8,128)(2,1)}, bf16[256,512]{1,0:T(8,128)(2,1)}, bf16[256,1024]{1,0:T(8,128)(2,1)}) async-done(((bf16[256,1024]{1,0:T(8,128)(2,1)}, bf16[256,512]{1,0:T(8,128)(2,1)}, bf16[256,512]{1,0:T(8,128)(2,1)}, bf16[256,1024]{1,0:T(8,128)(2,1)}), (bf16[256,1024]{1,0:T(8,128)(2,1)}, bf16[256,512]{1,0:T(8,128)(2,1)}, ...) | async-done | bytes 1572880 | tf_op jit(solution)/shard_map/psum | solution.py:401
  1628.9 2.2 convert_element_type.306
  (503 shorter events, 197.4 us)
Async XLA Ops:
  7.2 27.2 %copy-start.1 = (bf16[1,128,1024]{2,1,0:T(8,128)(2,1)S(1)}, bf16[1,128,1024]{2,1,0:T(8,128)(2,1)}, u32[]{:S(2)}) copy-start(bf16[1,128,1024]{2,1,0:T(8,128)(2,1)} %param.22) | copy-start | bytes 786436
  7.2 25.7 %all-gather.12.cloned.1.call-start = ((), (), s32[]{:S(2)}) async-start(), calls=%async_computation.14 | async-start | bytes 1310720 | tf_op jit(solution)/shard_map/all_gather | solution.py:132
  7.9 48.3 %all-gather.18.cloned.1.call-start = ((), (), s32[]{:S(2)}) async-start(), calls=%async_computation.17 | async-start | bytes 1310720 | tf_op jit(solution)/shard_map/all_gather | solution.py:133
  8.7 79.1 %all-gather.16.cloned.1.call-start = ((), (), s32[]{:S(2)}) async-start(), calls=%async_computation.16 | async-start | bytes 2621440 | tf_op jit(solution)/shard_map/all_gather | solution.py:131
  9.4 164.4 %all-gather.14.cloned.1.call-start = ((), (), s32[]{:S(2)}) async-start(), calls=%async_computation.15 | async-start | bytes 4325376 | tf_op jit(solution)/shard_map/all_gather | solution.py:167
  15.2 75.4 %copy-start.27 = (f32[4,1,256]{2,1,0:T(1,128)}, f32[4,1,256]{2,1,0:T(1,128)S(1)}, u32[]{:S(2)}) copy-start(f32[4,1,256]{2,1,0:T(1,128)S(1)} %convert_element_type.330) | copy-start | bytes 12292
  16.8 74.7 %copy-start.21 = (f32[128,64]{0,1:T(8,128)}, f32[128,64]{0,1:T(8,128)S(1)}, u32[]{:S(2)}) copy-start(f32[128,64]{0,1:T(8,128)S(1)} %get-tuple-element.1117) | copy-start | bytes 98308
  16.8 74.7 %copy-start.24 = (f32[128,64]{0,1:T(8,128)}, f32[128,64]{0,1:T(8,128)S(1)}, u32[]{:S(2)}) copy-start(f32[128,64]{0,1:T(8,128)S(1)} %get-tuple-element.1116) | copy-start | bytes 98308
  17.9 72.7 %copy-start.36 = (f32[128]{0:T(128)}, f32[128]{0:T(128)S(1)}, u32[]{:S(2)}) copy-start(f32[128]{0:T(128)S(1)} %add_rsqrt_fusion.1) | copy-start | bytes 1540
  32.9 26.2 %copy-start.34 = (s32[1,128,8]{1,2,0:T(8,128)S(1)}, s32[1,128,8]{1,2,0:T(8,128)}, u32[]{:S(2)}) copy-start(s32[1,128,8]{1,2,0:T(8,128)} %param.23) | copy-start | bytes 12292
  34.4 25.0 %copy-start.51 = (bf16[256]{0:T(256)(128)(2,1)S(1)}, bf16[256]{0:T(256)(128)(2,1)}, u32[]{:S(2)}) copy-start(bf16[256]{0:T(256)(128)(2,1)} %param.30) | copy-start | bytes 1540
  34.4 30.1 %copy-start.47 = (s32[32]{0:T(128)S(1)}, s32[32]{0:T(128)}, u32[]{:S(2)}) copy-start(s32[32]{0:T(128)} %param.24) | copy-start | bytes 388
  35.7 221.4 %all-gather.20.cloned.1.call-start = ((), (), s32[]{:S(2)}) async-start(), calls=%async_computation.18 | async-start | bytes 4325376 | tf_op jit(solution)/shard_map/all_gather | solution.py:168
  58.5 230.6 %all-gather.22.cloned.1.call-start = ((), (), s32[]{:S(2)}) async-start(), calls=%async_computation.19 | async-start | bytes 2621440 | tf_op jit(solution)/shard_map/all_gather | solution.py:134
  64.5 226.9 %copy-start.32 = (f32[4,1,256]{2,1,0:T(1,128)}, f32[4,1,256]{2,1,0:T(1,128)S(1)}, u32[]{:S(2)}) copy-start(f32[4,1,256]{2,1,0:T(1,128)S(1)} %convert_element_type.331) | copy-start | bytes 12292
  74.4 275.6 %copy-start.39 = (s32[1024,1]{0,1:T(1,128)}, s32[1024,1]{0,1:T(1,128)S(1)}, u32[]{:S(2)}) copy-start(s32[1024,1]{0,1:T(1,128)S(1)} %compare_select_fusion) | copy-start | bytes 12292
  288.9 11.3 copy-start.29
  288.9 11.3 copy-start.43
  288.9 11.3 copy-start.48
  289.0 11.2 copy-start.13
  291.3 8.9 copy-start.45
  292.2 56.7 %copy-start.11 = (bf16[128,1024]{1,0:T(8,128)(2,1)}, bf16[128,1024]{1,0:T(8,128)(2,1)S(1)}, u32[]{:S(2)}) copy-start(bf16[128,1024]{1,0:T(8,128)(2,1)S(1)} %multiply_convert_fusion.1) | copy-start | bytes 786436
  300.2 6.6 copy-start.38
  300.2 48.7 %copy-start.19 = (bf16[1,128,1024]{2,1,0:T(8,128)(2,1)S(1)}, bf16[1,128,1024]{2,1,0:T(8,128)(2,1)}, u32[]{:S(2)}) copy-start(bf16[1,128,1024]{2,1,0:T(8,128)(2,1)} %param.35) | copy-start | bytes 786436
  300.3 57.5 %all-to-all-start = ((bf16[32,48,1024]{2,1,0:T(8,128)(2,1)}), bf16[32,48,1024]{2,1,0:T(8,128)(2,1)}, u32[]{:S(2)}, u32[]{:S(2)}) async-start(bf16[32,48,1024]{2,1,0:T(8,128)(2,1)} %bitcast.20), calls=%async_computation | async-start | bytes 6291456 | tf_op jit(solution)/shard_map/all_to_all | solution.py:230
  306.1 69.4 %all-gather.26.cloned.1.call-start = ((), (), s32[]{:S(2)}) async-start(), calls=%async_computation.21 | async-start | bytes 1310720 | tf_op jit(solution)/shard_map/all_gather | solution.py:140
  349.0 8.8 copy-start.8
  349.2 8.5 copy-start.40
  357.8 61.3 %all-to-all-start.2 = ((bf16[32,48,1024]{2,1,0:T(8,128)(2,1)}), bf16[32,48,1024]{2,1,0:T(8,128)(2,1)}, u32[]{:S(2)}, u32[]{:S(2)}) async-start(bf16[32,48,1024]{2,1,0:T(8,128)(2,1)} %bitcast.42), calls=%async_computation.2 | async-start | bytes 6291456 | tf_op jit(solution)/shard_map/all_to_all | solution.py:267
  373.9 44.9 %all-gather.28.cloned.1.call-start = ((), (), s32[]{:S(2)}) async-start(), calls=%async_computation.22 | async-start | bytes 1310720 | tf_op jit(solution)/shard_map/all_gather | solution.py:141
  374.7 69.2 %all-gather.24.cloned.1.call-start = ((), (), s32[]{:S(2)}) async-start(), calls=%async_computation.20 | async-start | bytes 1310720 | tf_op jit(solution)/shard_map/all_gather | solution.py:139
  424.8 28.3 %copy-start.50 = (bf16[1,512,1024]{2,1,0:T(8,128)(2,1)S(1)}, bf16[1,512,1024]{2,1,0:T(8,128)(2,1)}, u32[]{:S(2)}) copy-start(bf16[1,512,1024]{2,1,0:T(8,128)(2,1)} %all-gather.28.cloned.1.call-done) | copy-start | bytes 3145732
  453.0 3.5 copy-start.53
  456.5 51.2 %all-to-all-start.1 = ((bf16[32,48,1024]{2,1,0:T(8,128)(2,1)}), bf16[32,48,1024]{2,1,0:T(8,128)(2,1)S(1)}, u32[]{:S(2)}, u32[]{:S(2)}) async-start(bf16[32,48,1024]{2,1,0:T(8,128)(2,1)} %convolution_convert_fusion), calls=%async_computation.1 | async-start | bytes 6291456 | tf_op jit(solution)/shard_map/all_to_all | solution.py:239
  465.9 3.8 copy-start.16
  465.9 3.8 copy-start.18
  509.4 49.6 %all-to-all-start.3 = ((bf16[32,48,1024]{2,1,0:T(8,128)(2,1)}), bf16[32,48,1024]{2,1,0:T(8,128)(2,1)S(1)}, u32[]{:S(2)}, u32[]{:S(2)}) async-start(bf16[32,48,1024]{2,1,0:T(8,128)(2,1)} %add_convert_fusion), calls=%async_computation.3 | async-start | bytes 6291456 | tf_op jit(solution)/shard_map/all_to_all | solution.py:282
  517.6 366.2 %reduce-scatter.33.cloned.1.call-start = ((), (), s32[]{:S(2)}) async-start(), calls=%async_computation.32 | async-start | bytes 4325376
  518.6 8.3 copy-start.35
  559.0 8.9 copy-start.33
  559.0 8.9 copy-start.46
  564.8 5.2 copy-start.7
  564.8 5.2 copy-start.15
  564.8 5.2 copy-start.20
  564.8 6.2 copy-start.5
  689.9 383.8 %reduce-scatter.31.cloned.1.call-start = ((), (), s32[]{:S(2)}) async-start(), calls=%async_computation.31 | async-start | bytes 4325376
  696.5 5.4 copy-start.17
  696.5 394.0 %reduce-scatter.29.cloned.1.call-start = ((), (), s32[]{:S(2)}) async-start(), calls=%async_computation.30 | async-start | bytes 1310720 | tf_op jit(solution)/shard_map/reduce_scatter | solution.py:415
  701.9 412.4 %reduce-scatter.27.cloned.1.call-start = ((), (), s32[]{:S(2)}) async-start(), calls=%async_computation.29 | async-start | bytes 1310720 | tf_op jit(solution)/shard_map/reduce_scatter | solution.py:412
  706.6 5.3 copy-start.14
  706.7 431.2 %reduce-scatter.25.cloned.1.call-start = ((), (), s32[]{:S(2)}) async-start(), calls=%async_computation.28 | async-start | bytes 1310720 | tf_op jit(solution)/shard_map/reduce_scatter | solution.py:409
  711.9 457.7 %reduce-scatter.21.cloned.1.call-start = ((), (), s32[]{:S(2)}) async-start(), calls=%async_computation.26 | async-start | bytes 2621440 | tf_op jit(solution)/shard_map/reduce_scatter | solution.py:389
  714.1 487.0 %reduce-scatter.15.cloned.1.call-start = ((), (), s32[]{:S(2)}) async-start(), calls=%async_computation.23 | async-start | bytes 2621440 | tf_op jit(solution)/shard_map/reduce_scatter | solution.py:380
  715.7 359.1 %copy-start.25 = (f32[128,64]{0,1:T(8,128)S(1)}, f32[128,64]{0,1:T(8,128)}, u32[]{:S(2)}) copy-start(f32[128,64]{0,1:T(8,128)} %copy-done.24) | copy-start | bytes 98308
  717.9 357.0 %copy-start.22 = (f32[128,64]{0,1:T(8,128)S(1)}, f32[128,64]{0,1:T(8,128)}, u32[]{:S(2)}) copy-start(f32[128,64]{0,1:T(8,128)} %copy-done.21) | copy-start | bytes 98308
  717.9 507.3 %reduce-scatter.19.cloned.1.call-start = ((), (), s32[]{:S(2)}) async-start(), calls=%async_computation.25 | async-start | bytes 1310720 | tf_op jit(solution)/shard_map/reduce_scatter | solution.py:386
  886.2 190.3 %copy-start.12 = (bf16[128,1024]{1,0:T(8,128)(2,1)S(1)}, bf16[128,1024]{1,0:T(8,128)(2,1)}, u32[]{:S(2)}) copy-start(bf16[128,1024]{1,0:T(8,128)(2,1)} %copy-done.11) | copy-start | bytes 786436
  886.2 191.5 %copy-start.52 = (u32[128]{0:T(128)S(1)}, u32[128]{0:T(128)}, u32[]{:S(2)}) copy-start(u32[128]{0:T(128)} %constant.309) | copy-start | bytes 1540
  886.3 362.9 %reduce-scatter.17.cloned.1.call-start = ((), (), s32[]{:S(2)}) async-start(), calls=%async_computation.24 | async-start | bytes 1310720 | tf_op jit(solution)/shard_map/reduce_scatter | solution.py:383
  1076.5 193.8 %reduce-scatter.23.cloned.1.call-start = ((), (), s32[]{:S(2)}) async-start(), calls=%async_computation.27 | async-start | bytes 81920 | tf_op jit(solution)/shard_map/reduce_scatter | solution.py:395
  1077.4 551.5 %all-reduce.7.cloned.1.call-start = ((), (), s32[]{:S(2)}) async-start(), calls=%async_computation.33 | async-start | bytes 3145728 | tf_op jit(solution)/shard_map/psum | solution.py:401
  1079.0 171.6 %copy-start.4 = (bf16[1024,1024]{1,0:T(8,128)(2,1)S(1)}, bf16[1024,1024]{1,0:T(8,128)(2,1)}, u32[]{:S(2)}) copy-start(bf16[1024,1024]{1,0:T(8,128)(2,1)} %all-gather.16.cloned.1.call-done) | copy-start | bytes 6291460
  1249.3 2.6 copy-start.10
  1628.9 5.8 copy-start.23
  (14 other events, 24.4 us)
Sparse Core Ops, SparseCore 0:
  9.7 23.1 all-gather.11
  34.5 21.6 all-gather.17
  57.9 29.8 all-gather.15
  90.9 82.8 all-gather.13
  177.4 79.6 all-gather.19
  258.6 26.6 all-gather.21
  308.6 42.7 all-gather.25
  376.4 42.3 all-gather.27
  420.5 23.3 all-gather.23
  690.0 193.7 reduce-scatter.32
  886.2 187.4 reduce-scatter.30
  1076.0 14.3 reduce-scatter.28
  1093.0 21.2 reduce-scatter.26
  1116.5 21.2 reduce-scatter.24
  1140.2 29.3 reduce-scatter.20
  1171.9 29.1 reduce-scatter.14
  1204.1 21.1 reduce-scatter.18
  1228.1 21.1 reduce-scatter.16
  1252.3 18.0 reduce-scatter.22
  1272.9 355.9 all-reduce.6
where the time goes:
time: 1650 us; the launch traced here: 1640 us
  waiting for transfers between devices  1010 us (61%)
  blocking collectives  242 us (15%)
  matrix products  140 us (8%)
  local copies, waits for them, and re-layouts  128 us (8%)
  other arithmetic  61.1 us (4%)
  starting transfers between devices  41 us (2%)
  between operations  16.5 us (1%)
    unnamed x22, waiting for transfers between devices  358 us
    psum x1, blocking collectives, on_device(): lax.psum(dense_sums[0].astype(jnp.bfloat16), 'ctx').astype(jnp.float32)  183 us
    psum x1, waiting for transfers between devices, on_device(): lax.psum(dense_sums[1].astype(jnp.bfloat16), 'ctx').astype(jnp.float32)  172 us
    dot_general x81, matrix products, contract(): return jnp.einsum(form, left, right, preferred_element_type=jnp.float32)  121 us
    all_gather x1, waiting for transfers between devices, on_device(): lax.all_gather(key_rot, 'ctx', axis=0, tiled=True)  82.2 us
    all_gather x1, waiting for transfers between devices, on_device(): lax.all_gather(value_rows, 'ctx', axis=0, tiled=True)  58.2 us
    all_gather x1, blocking collectives, on_device(): lax.all_gather(w_router, 'fsdp', axis=0, tiled=True)  42.1 us
    all_gather x1, waiting for transfers between devices, on_device(): lax.all_gather(w_down, 'fsdp', axis=1, tiled=True)  37.7 us
  transfers between devices with their start and end apart: 24, of which 21 were waited for; matrix products, arithmetic and copies ran while one was open for 10% of the time, Pallas kernels for 0%

commit v1 on v0

v1 whole, which is shorter than its diff:
```python
import functools

import jax
import jax.numpy as jnp
from jax import lax
from jax.experimental import pallas as pl
from jax.experimental.pallas import tpu as pltpu
from jax.sharding import Mesh
from jax.sharding import PartitionSpec as P

HEADS = 16
KV_HEADS = 8
HEAD_DIM = 64
EXPERTS = 32
TOP = 8
CAP = 48
HALF = 64
TILE = 512

epsilon = 1e-06
attn_scale = 0.015625
residual_scale = 0.22
masked_value = -1e30

CTX = ("x", "z", "yh")
ZY = ("z", "yh")
EVERY = ("x", "z", "yh", "yl", "core")
bf16 = jnp.bfloat16
f32 = jnp.float32


def product(left, right):
    return jnp.dot(left, right, preferred_element_type=f32)


def product_nt(left, right):
    return lax.dot_general(left, right, (((1,), (1,)), ((), ())), preferred_element_type=f32)


def product_tn(left, right):
    return lax.dot_general(left, right, (((0,), (0,)), ((), ())), preferred_element_type=f32)


def swap(values, axis):
    return lax.ppermute(values, axis, [(0, 1), (1, 0)])


def turn(values, axis, step):
    return lax.ppermute(values, axis, [(i, (i + step) % 4) for i in range(4)])


def exchange(values, axes):
    return lax.all_to_all(values, axes, 0, 0, tiled=True)


def after(values, *others):
    return lax.optimization_barrier((values,) + others)[0]


def gather_fsdp(shard):
    row, core = lax.axis_index("yl"), lax.axis_index("core")
    pair = jnp.zeros((2, 2) + shard.shape, shard.dtype)
    zero = (0,) * shard.ndim
    other = swap(shard, "yl")
    mine = lax.dynamic_update_slice(jnp.zeros((2,) + shard.shape, shard.dtype), shard[None], (row,) + zero)
    mine = lax.dynamic_update_slice(mine, other[None], (1 - row,) + zero)
    theirs = swap(mine, "core")
    pair = lax.dynamic_update_slice(pair, mine[:, None], (0, core) + zero)
    pair = lax.dynamic_update_slice(pair, theirs[:, None], (0, 1 - core) + zero)
    return pair.reshape((4,) + shard.shape)


def scatter_fsdp(parts):
    row, core = lax.axis_index("yl"), lax.axis_index("core")
    parts = parts.astype(bf16).reshape((2, 2) + parts.shape[1:])
    away = lax.dynamic_index_in_dim(parts, 1 - core, 1, keepdims=False)
    keep = lax.dynamic_index_in_dim(parts, core, 1, keepdims=False)
    both = keep.astype(f32) + swap(away, "core").astype(f32)
    away = lax.dynamic_index_in_dim(both, 1 - row, 0, keepdims=False).astype(bf16)
    keep = lax.dynamic_index_in_dim(both, row, 0, keepdims=False)
    return keep + swap(away, "yl").astype(f32)


def rope_tables(positions):
    freqs = jnp.power(10000.0, -jnp.arange(0, HEAD_DIM, 2, dtype=f32) / HEAD_DIM)
    angles = positions.astype(f32)[:, None] * freqs[None, :]
    angles = jnp.concatenate([angles, angles], axis=-1)
    return (jnp.cos(angles), jnp.sin(angles))


def rotate(values, cosine, sine):
    middle = HEAD_DIM // 2
    turned = jnp.concatenate([-values[..., middle:], values[..., :middle]], axis=-1)
    return values * cosine + turned * sine


def rotate_back(grads, cosine, sine):
    middle = HEAD_DIM // 2
    scaled = grads * sine
    turned = jnp.concatenate([scaled[..., middle:], -scaled[..., :middle]], axis=-1)
    return grads * cosine + turned


def norm_back(values, inv_rms, gain, grad):
    weighted = grad * gain
    gain_grad = jnp.sum(grad * values * inv_rms, axis=0)
    inner_mean = jnp.mean(weighted * values, axis=-1, keepdims=True)
    return (weighted * inv_rms - values * inv_rms * inv_rms * inv_rms * inner_mean, gain_grad)


def half(index):
    return pl.ds(pl.multiple_of(index * HALF, HALF), HALF)


def key_tile(counter):
    return pl.ds(pl.multiple_of(counter * TILE, TILE), TILE)


def sort_keys(knum_ref, kv_refs, kvs, kvt):
    blocks = kv_refs[0].shape[0] // HALF
    for slot, kv_ref in enumerate(kv_refs):
        for block in range(blocks):
            kvs[half(knum_ref[slot * blocks + block]), :] = kv_ref[block * HALF : (block + 1) * HALF, :]
    for tile in range(kvs.shape[0] // TILE):
        part = kvs[tile * TILE : (tile + 1) * TILE, :].astype(f32)
        kvt[:, tile * TILE : (tile + 1) * TILE] = part.T.astype(bf16)


def pair_rows(ref, first, second):
    return jnp.concatenate(
        [ref[0, half(first), :], ref[1, half(first), :], ref[0, half(second), :], ref[1, half(second), :]],
        axis=0,
    )


def pair_positions(low_number, high_number):
    column = lax.broadcasted_iota(jnp.int32, (1, 4 * HALF), 1)
    return jnp.where(column < 2 * HALF, low_number, high_number) * HALF + column % HALF


def score_tile(keys, queries, counter, positions, masked):
    scores = product_nt(keys, queries)
    if masked:
        key_pos = counter * TILE + lax.broadcasted_iota(jnp.int32, scores.shape, 0)
        scores = jnp.where(key_pos <= positions, scores, masked_value)
    return scores


def store_rows(ref, turned, first, second):
    rows = turned.T
    ref[half(first), :] = jnp.concatenate([rows[:HALF], rows[HALF : 2 * HALF]], axis=1).astype(ref.dtype)
    ref[half(second), :] = jnp.concatenate([rows[2 * HALF : 3 * HALF], rows[3 * HALF :]], axis=1).astype(ref.dtype)


def attend_kernel(order_ref, qnum_ref, knum_ref, q_ref, kv0, kv1, kv2, kv3, out_ref, turned_ref, lse_ref, kvs, kvt):
    sort_keys(knum_ref, (kv0, kv1, kv2, kv3), kvs, kvt)
    width = 4 * HALF

    @pl.loop(0, q_ref.shape[1] // (2 * HALF))
    def _(pair):
        first, second = order_ref[2 * pair], order_ref[2 * pair + 1]
        low_number, high_number = qnum_ref[first], qnum_ref[second]
        queries = pair_rows(q_ref, first, second)
        positions = pair_positions(low_number, high_number)

        def step(masked, counter, running):
            top, total, mixed = running
            scores = score_tile(kvs[key_tile(counter), :], queries, counter, positions, masked)
            new_top = jnp.maximum(top, jnp.max(scores, axis=0, keepdims=True))
            probs = jnp.exp(scores - new_top)
            shrink = jnp.exp(top - new_top)
            total = total * shrink + jnp.sum(probs, axis=0, keepdims=True)
            mixed = mixed * shrink + product(kvt[HEAD_DIM:, key_tile(counter)], probs.astype(bf16))
            return (new_top, total, mixed)

        start = (
            jnp.full((1, width), masked_value, f32),
            jnp.zeros((1, width), f32),
            jnp.zeros((HEAD_DIM, width), f32),
        )
        full = (low_number * HALF) // TILE
        last = (high_number * HALF) // TILE + 1
        running = lax.fori_loop(0, full, functools.partial(step, False), start)
        top, total, mixed = lax.fori_loop(full, last, functools.partial(step, True), running)
        mixed = mixed / total
        turned_ref[pair] = mixed
        lse_ref[pair] = top + jnp.log(total)
        store_rows(out_ref, mixed, first, second)


def attend_grad_kernel(
    order_ref, qnum_ref, knum_ref, q_ref, kv0, kv1, kv2, kv3, grad_ref, turned_ref, lse_ref,
    dq_ref, dkv0, dkv1, dkv2, dkv3, kvs, kvt, total_ref,
):
    sort_keys(knum_ref, (kv0, kv1, kv2, kv3), kvs, kvt)
    total_ref[...] = jnp.zeros_like(total_ref)
    width = 4 * HALF

    @pl.loop(0, q_ref.shape[1] // (2 * HALF))
    def _(pair):
        first, second = order_ref[2 * pair], order_ref[2 * pair + 1]
        low_number, high_number = qnum_ref[first], qnum_ref[second]
        queries = pair_rows(q_ref, first, second)
        grads = pair_rows(grad_ref, first, second)
        both = jnp.concatenate([queries, grads], axis=0)
        positions = pair_positions(low_number, high_number)
        lse = lse_ref[pair]
        dots = jnp.sum(grads.astype(f32).T[HEAD_DIM:] * turned_ref[pair], axis=0, keepdims=True)

        def step(masked, counter, query_acc):
            keys = kvs[key_tile(counter), :]
            probs = jnp.exp(score_tile(keys, queries, counter, positions, masked) - lse)
            score_grad = (probs * (product_nt(keys, grads) - dots)).astype(bf16)
            sides = jnp.concatenate([score_grad, probs.astype(bf16)], axis=1)
            total_ref[key_tile(counter), :] += product(sides, both)
            return query_acc + product(kvt[:HEAD_DIM, key_tile(counter)], score_grad)

        full = (low_number * HALF) // TILE
        last = (high_number * HALF) // TILE + 1
        query_acc = lax.fori_loop(0, full, functools.partial(step, False), jnp.zeros((HEAD_DIM, width), f32))
        query_acc = lax.fori_loop(full, last, functools.partial(step, True), query_acc)
        store_rows(dq_ref, query_acc * attn_scale, first, second)

    blocks = dkv0.shape[0] // HALF
    for slot, dkv in enumerate((dkv0, dkv1, dkv2, dkv3)):
        for block in range(blocks):
            dkv[block * HALF : (block + 1) * HALF, :] = total_ref[
                half(knum_ref[slot * blocks + block]), :
            ].astype(bf16)


SMEM = pl.BlockSpec(memory_space=pltpu.SMEM)
VMEM = pl.BlockSpec(memory_space=pltpu.VMEM)


def attend(numbers, queries, kv_parts):
    rows = queries.shape[1]
    keys = rows * len(kv_parts)
    pairs = rows // (2 * HALF)
    return pl.pallas_call(
        attend_kernel,
        out_shape=(
            jax.ShapeDtypeStruct((rows, 2 * HEAD_DIM), bf16),
            jax.ShapeDtypeStruct((pairs, HEAD_DIM, 4 * HALF), f32),
            jax.ShapeDtypeStruct((pairs, 1, 4 * HALF), f32),
        ),
        in_specs=[SMEM] * 3 + [VMEM] * 5,
        out_specs=(VMEM,) * 3,
        scratch_shapes=[pltpu.VMEM((keys, 2 * HEAD_DIM), bf16), pltpu.VMEM((2 * HEAD_DIM, keys), bf16)],
        compiler_params=pltpu.CompilerParams(vmem_limit_bytes=40 * 1024 * 1024),
        cost_estimate=pl.CostEstimate(flops=12_000_000_000, bytes_accessed=4_000_000, transcendentals=5_000_000),
    )(*numbers, queries, *kv_parts)


def attend_grad(numbers, queries, kv_parts, grads, turned, lse):
    rows = queries.shape[1]
    keys = rows * len(kv_parts)
    return pl.pallas_call(
        attend_grad_kernel,
        out_shape=(jax.ShapeDtypeStruct((rows, 2 * HEAD_DIM), f32),)
        + (jax.ShapeDtypeStruct((rows, 2 * HEAD_DIM), bf16),) * 4,
        in_specs=[SMEM] * 3 + [VMEM] * 8,
        out_specs=(VMEM,) * 5,
        scratch_shapes=[
            pltpu.VMEM((keys, 2 * HEAD_DIM), bf16),
            pltpu.VMEM((2 * HEAD_DIM, keys), bf16),
            pltpu.VMEM((keys, 2 * HEAD_DIM), f32),
        ],
        compiler_params=pltpu.CompilerParams(vmem_limit_bytes=40 * 1024 * 1024),
        cost_estimate=pl.CostEstimate(flops=30_000_000_000, bytes_accessed=6_000_000, transcendentals=5_000_000),
    )(*numbers, queries, *kv_parts, grads, turned, lse)


def block_numbers(block_pairs):
    place = lax.axis_index("x")
    groups = block_pairs.reshape(4, 8)
    groups = groups[(place - jnp.arange(4)) % 4]
    numbers = jnp.stack([groups, 63 - groups], axis=-1).reshape(-1)
    own = numbers[:16]
    rank = jnp.sum((own[None, :] < own[:, None]).astype(jnp.int32), axis=1)
    spots = jnp.arange(16, dtype=jnp.int32)
    order = jnp.sum(jnp.where(rank[None, :] == spots[:, None], spots[None, :], 0), axis=1)
    return (order, own, numbers)


def on_device(
    block_input,
    routes,
    block_pairs,
    norm1_gain,
    w_query,
    w_key,
    w_value,
    w_out,
    norm2_gain,
    w_router,
    w_gate,
    w_up,
    w_down,
    cotangent,
):
    tokens, width = block_input.shape[1:]
    head = lax.axis_index(ZY)
    expert = lax.axis_index(CTX)
    shard_rows = w_query.shape[0]
    own_input = block_input[0]

    group_input = exchange(jnp.tile(own_input, (KV_HEADS, 1)), ZY)
    by_head = jnp.concatenate(
        [
            w_query.reshape(shard_rows, KV_HEADS, 2 * HEAD_DIM),
            w_key.reshape(shard_rows, KV_HEADS, HEAD_DIM),
            w_value.reshape(shard_rows, KV_HEADS, HEAD_DIM),
        ],
        axis=2,
    )
    head_shard = lax.dynamic_index_in_dim(by_head, head, 1, keepdims=False)
    gains = jnp.stack([norm1_gain, norm2_gain])
    head_w = gather_fsdp(head_shard).reshape(width, 4 * HEAD_DIM)
    gains = gather_fsdp(gains)
    gain_one = gains[:, 0].reshape(width).astype(f32)
    gain_two = gains[:, 1].reshape(width).astype(f32)

    numbers = block_numbers(block_pairs)
    group_pos = (numbers[1][:, None] * HALF + jnp.arange(HALF, dtype=jnp.int32)[None, :]).reshape(-1)
    cosine, sine = rope_tables(group_pos)

    chosen = routes[0]
    uses = jnp.sum(
        (chosen[:, :, None] == jnp.arange(EXPERTS, dtype=jnp.int32)[None, None, :]).astype(f32), axis=1
    )
    earlier = jnp.tril(jnp.ones((tokens, tokens), bf16), -1)
    rank = product(earlier, uses.astype(bf16)).astype(jnp.int32)
    rank = jnp.where(uses > 0, rank, -1)
    slot_of = (
        rank.T[:, None, :] == jnp.arange(CAP, dtype=jnp.int32)[None, :, None]
    )
    send = slot_of.astype(bf16).reshape(EXPERTS * CAP, tokens)

    group_f = group_input.astype(f32)
    group_inv = lax.rsqrt(jnp.mean(group_f * group_f, axis=-1, keepdims=True) + epsilon)
    group_normed = (group_f * group_inv * gain_one).astype(bf16)
    projected = product(group_normed, head_w)
    key_rot = rotate(projected[:, 2 * HEAD_DIM : 3 * HEAD_DIM], cosine, sine)
    kv_own = jnp.concatenate([key_rot, projected[:, 3 * HEAD_DIM :]], axis=1).astype(bf16)
    kv_parts = [kv_own] + [turn(kv_own, "x", step) for step in (1, 2, 3)]
    queries = jnp.stack(
        [
            rotate(projected[:, :HEAD_DIM], cosine, sine),
            rotate(projected[:, HEAD_DIM : 2 * HEAD_DIM], cosine, sine),
        ]
    ).astype(bf16) * bf16(attn_scale)
    queries = jnp.pad(queries, ((0, 0), (0, 0), (0, HEAD_DIM)))

    shard_out, shard_router, shard_gu, shard_down, cot_rows, by_head = lax.optimization_barrier(
        (w_out, w_router, jnp.concatenate([w_gate[0], w_up[0]], axis=1), w_down[0], cotangent[0], by_head, kv_own)
    )[:6]
    out_w = gather_fsdp(shard_out).reshape(HEADS * HEAD_DIM, width)
    router_w = gather_fsdp(shard_router).reshape(width, EXPERTS)
    gu_w = gather_fsdp(shard_gu).reshape(width, -1)
    down_w = gather_fsdp(shard_down).reshape(-1, width)
    marked = jnp.concatenate(
        [cot_rows, uses.astype(bf16), jnp.zeros((tokens, 128 - EXPERTS), bf16)], axis=1
    )
    marked_arrived = exchange(product(send, marked).astype(bf16), CTX)

    attn_group, attn_turned, lse = attend(numbers, queries, kv_parts)

    attn_rows = exchange(attn_group, ZY).reshape(KV_HEADS, tokens, 2 * HEAD_DIM)
    attn_rows = attn_rows.transpose(1, 0, 2).reshape(tokens, HEADS * HEAD_DIM)
    inputs = own_input.astype(f32)
    hidden = inputs + residual_scale * product(attn_rows, out_w)
    inv_rms2 = lax.rsqrt(jnp.mean(hidden * hidden, axis=-1, keepdims=True) + epsilon)
    normed2 = (hidden * inv_rms2 * gain_two).astype(bf16)

    def gate_of(rows, mask):
        logits = jnp.where(mask > 0, product(rows, router_w), masked_value)
        exps = jnp.where(mask > 0, jnp.exp(logits - jnp.max(logits, axis=-1, keepdims=True)), 0.0)
        return exps / jnp.maximum(jnp.sum(exps, axis=-1, keepdims=True), 1e-30)

    arrived = exchange(product(send, normed2).astype(bf16), CTX)
    gate_probs = gate_of(normed2, uses)

    cot_arrived = marked_arrived[:, :width]
    uses_arrived = marked_arrived[:, width : width + EXPERTS].astype(f32)
    hidden_units = down_w.shape[0]
    pre = product(arrived, gu_w)
    gate_pre, up_pre = pre[:, :hidden_units], pre[:, hidden_units:]
    sigmoid_a = jax.nn.sigmoid(gate_pre)
    swish_act = gate_pre * sigmoid_a
    inner_act = (swish_act * up_pre).astype(bf16)
    expert_out = product(inner_act, down_w).astype(bf16)
    slot_probs = jnp.sum(
        jnp.where(jnp.arange(EXPERTS)[None, :] == expert, gate_of(arrived, uses_arrived), 0.0),
        axis=1,
        keepdims=True,
    )
    mix_grad = residual_scale * cot_arrived.astype(f32)
    slot_gate_grad = jnp.sum(mix_grad * expert_out.astype(f32), axis=1)
    route_grad = (slot_probs * mix_grad).astype(bf16)
    inner_grad = product_nt(route_grad, down_w)
    pre_grad = jnp.concatenate(
        [
            (inner_grad * up_pre * sigmoid_a * (1.0 + gate_pre * (1.0 - sigmoid_a))).astype(bf16),
            (inner_grad * swish_act).astype(bf16),
        ],
        axis=1,
    )
    expert_in_grad = product_nt(pre_grad, gu_w).astype(bf16)
    gate_grad_back = exchange(slot_gate_grad.reshape(EXPERTS, CAP), CTX)
    back = exchange(expert_in_grad, CTX)

    gate_grad = jnp.sum(jnp.where(slot_of, gate_grad_back[:, :, None], 0.0), axis=1).T
    mean_grad = jnp.sum(gate_probs * gate_grad, axis=-1, keepdims=True)
    logit_grad = (gate_probs * (gate_grad - mean_grad)).astype(bf16)
    normed2_grad = product_tn(send, back) + product_nt(logit_grad, router_w)
    hidden_part, gain_two_grad = norm_back(hidden, inv_rms2, gain_two, normed2_grad)
    hidden_grad = cotangent[0].astype(f32) + hidden_part
    branch_grad = (residual_scale * hidden_grad).astype(bf16)
    attn_grad = product_nt(branch_grad, out_w).astype(bf16)

    attn_grad = attn_grad.reshape(tokens, KV_HEADS, 2 * HEAD_DIM).transpose(1, 0, 2)
    group_grad = exchange(attn_grad.reshape(KV_HEADS * tokens, 2 * HEAD_DIM), ZY)
    group_grad = group_grad.reshape(KV_HEADS * tokens, 2, HEAD_DIM).transpose(1, 0, 2)
    group_grad_pad = jnp.pad(group_grad, ((0, 0), (0, 0), (HEAD_DIM, 0)))

    expert_out, pre_grad, inner_act, attn_rows_l, branch_grad_l, normed2_l, logit_grad_l, gain_two_grad, by_head = (
        lax.optimization_barrier(
            (expert_out, pre_grad, inner_act, attn_rows, branch_grad, normed2, logit_grad, gain_two_grad, by_head, attn_grad)
        )[:9]
    )
    dq, *dkv_parts = attend_grad(numbers, queries, kv_parts, group_grad_pad, attn_turned, lse)
    returned = exchange(expert_out, CTX)
    grad_gu = product_tn(arrived, pre_grad).reshape(4, -1, 2 * hidden_units)
    grad_down = product_tn(inner_act, route_grad).reshape(4, -1, width)
    expert_sums = scatter_fsdp(jnp.concatenate([grad_gu, grad_down], axis=1))
    dense = jnp.concatenate(
        [
            product_tn(attn_rows_l, branch_grad_l),
            product_tn(normed2_l, logit_grad_l),
            gain_two_grad[:, None],
            jnp.zeros((width, 128 - EXPERTS - 1), f32),
        ],
        axis=1,
    )
    dense = scatter_fsdp(dense.reshape(4, width // 4, width + 128))
    dense = exchange(dense.astype(bf16), CTX).reshape(32, -1, width + 128)
    dense = jnp.sum(dense.astype(f32), axis=0).astype(bf16)
    dense = exchange(jnp.tile(dense, (32, 1)), CTX).astype(f32)
    full_w = gather_fsdp(by_head).reshape(width, -1)

    weights = jnp.where(slot_of, gate_probs.T[:, None, :], 0.0).reshape(EXPERTS * CAP, tokens)
    weights_hi = weights.astype(bf16)
    weights_lo = (weights - weights_hi.astype(f32)).astype(bf16)
    mixture = product_tn(weights_hi, returned) + product_tn(weights_lo, returned)
    output = hidden + residual_scale * mixture

    dkv = dkv_parts[0].astype(f32)
    for step in (1, 2, 3):
        dkv = dkv + turn(dkv_parts[step], "x", -step).astype(f32)
    grads = jnp.concatenate(
        [
            rotate_back(dq[:, :HEAD_DIM], cosine, sine),
            rotate_back(dq[:, HEAD_DIM:], cosine, sine),
            rotate_back(dkv[:, :HEAD_DIM], cosine, sine),
            dkv[:, HEAD_DIM:],
        ],
        axis=1,
    ).astype(bf16)
    token_grads = exchange(grads, ZY).reshape(KV_HEADS, tokens, 4 * HEAD_DIM)
    token_grads = token_grads.transpose(1, 0, 2).reshape(tokens, -1)
    head_grad = scatter_fsdp(product_tn(group_normed, grads).reshape(4, shard_rows, 4 * HEAD_DIM)).astype(bf16)
    head_sum = head_grad.astype(f32)
    for step in (1, 2, 3):
        head_sum = head_sum + turn(head_grad, "x", step).astype(f32)
    head_sum = exchange(jnp.tile(head_sum.astype(bf16), (KV_HEADS, 1)), ZY)
    head_sum = head_sum.reshape(KV_HEADS, shard_rows, 4 * HEAD_DIM).transpose(1, 0, 2).astype(f32)
    grad_query = head_sum[:, :, : 2 * HEAD_DIM].reshape(shard_rows, -1)
    grad_key = head_sum[:, :, 2 * HEAD_DIM : 3 * HEAD_DIM].reshape(shard_rows, -1)
    grad_value = head_sum[:, :, 3 * HEAD_DIM :].reshape(shard_rows, -1)

    normed1_grad = product_nt(token_grads, full_w)
    inv_rms1 = lax.rsqrt(jnp.mean(inputs * inputs, axis=-1, keepdims=True) + epsilon)
    input_part, gain_one_grad = norm_back(inputs, inv_rms1, gain_one, normed1_grad)
    input_grad = hidden_grad + input_part
    gain_one_grad = jnp.sum(exchange(jnp.tile(gain_one_grad.reshape(4, -1), (32, 1)), EVERY), axis=0)

    return (
        output.astype(bf16)[None],
        input_grad[None],
        gain_one_grad,
        grad_query,
        grad_key,
        grad_value,
        dense[:, :width],
        dense[:, width + EXPERTS],
        dense[:, width : width + EXPERTS],
        expert_sums[None, :shard_rows, :hidden_units],
        expert_sums[None, :shard_rows, hidden_units:],
        expert_sums[None, shard_rows:],
    )


def solution(mesh):
    fine = Mesh(mesh.devices.reshape(4, 4, 2, 2, 2), EVERY)
    rows, shards = P(("yl", "core"), CTX, None), P(("yl", "core"), None)
    gain, experts = P(("yl", "core")), P(CTX, ("yl", "core"), None)
    return jax.shard_map(
        on_device,
        mesh=fine,
        in_specs=(
            rows, rows, P(), gain, shards, shards, shards, shards, gain, shards, experts, experts, experts, rows,
        ),
        out_specs=(
            rows, rows, gain, shards, shards, shards, shards, gain, shards, experts, experts, experts,
        ),
        check_vma=False,
    )
```

time: 1650 us -> 646 us (0.39)
  waiting for transfers between devices: 1010 us -> 236 us
  blocking collectives: 242 us -> 0 us
  starting transfers between devices: 41 us -> 121 us
  matrix products: 140 us -> 70.1 us
  Pallas kernels: 0 us -> 42.3 us
  other arithmetic: 61.1 us -> 43.5 us
    unnamed x22 -> x0, waiting for transfers between devices: 358 us -> none
    all_gather x9 -> x0, waiting for transfers between devices: 246 us -> none  [the longest x1 82.2 us: on_device(): lax.all_gather(key_rot, 'ctx', axis=0, tiled=True)]
    psum x1 -> x0, blocking collectives: 183 us -> none  [on_device(): lax.psum(dense_sums[0].astype(jnp.bfloat16), 'ctx').astype(jnp.float32)]
    reduce_scatter x8 -> x0, waiting for transfers between devices: 176 us -> none  [the longest x1 31.4 us: on_device(): lax.psum_scatter(grad_query.astype(jnp.bfloat16), 'fsdp', scatter_dimensi...]
    psum x1 -> x0, waiting for transfers between devices: 172 us -> none  [on_device(): lax.psum(dense_sums[1].astype(jnp.bfloat16), 'ctx').astype(jnp.float32)]
    ppermute x0 -> x29, waiting for transfers between devices: none -> 112 us  [the longest x20 99.8 us: swap(): return lax.ppermute(values, axis, [(0, 1), (1, 0)])]
    dot_general x96 -> x22, matrix products: 140 us -> 70.1 us  [the longest x9 26 us: product(): return jnp.dot(left, right, preferred_element_type=f32)]
    all_to_all x4 -> x13, waiting for transfers between devices: 59.8 us -> 124 us  [exchange(): return lax.all_to_all(values, axes, 0, 0, tiled=True)]
  transfers between devices with their start and end apart: 24 -> 42, of which waited for: 21 -> 21; matrix products, arithmetic and copies ran while one was open for 10% -> 25% of each run, Pallas kernels for 0% -> 7%
where the time goes in v1:
time: 646 us; the launch traced here: 634 us
  waiting for transfers between devices  236 us (37%)
  starting transfers between devices  121 us (19%)
  local copies, waits for them, and re-layouts  119 us (18%)
  matrix products  70.1 us (11%)
  other arithmetic  43.5 us (7%)
  Pallas kernels  42.3 us (7%)
    all_to_all x13, waiting for transfers between devices, exchange(): return lax.all_to_all(values, axes, 0, 0, tiled=True)  124 us
    ppermute x20, waiting for transfers between devices, swap(): return lax.ppermute(values, axis, [(0, 1), (1, 0)])  99.8 us
    all_to_all x13, starting transfers between devices, exchange(): return lax.all_to_all(values, axes, 0, 0, tiled=True)  96.7 us
    unnamed x146, local copies, waits for them, and re-layouts  31.3 us
    dot_general x9, matrix products, product(): return jnp.dot(left, right, preferred_element_type=f32)  26 us
    dot_general x5, matrix products, product_nt(): lax.dot_general(left, right, (((1,), (1,)), ((), ())), preferred_element_...  24 us
    pallas_call x1, Pallas kernels, attend(): pl.pallas_call(attend_kernel, out_shape=(jax.ShapeDtypeStruct((rows, 2 *...  21.8 us
    pallas_call x1, Pallas kernels, attend_grad(): pl.pallas_call(attend_grad_kernel, out_shape=(jax.ShapeDtypeStruct((rows,...  20.6 us
  transfers between devices with their start and end apart: 42, of which 21 were waited for; matrix products, arithmetic and copies ran while one was open for 25% of the time, Pallas kernels for 7%

profile of v1, /device:TPU:0, one launch (start us, length us, event | category | flops | bytes accessed | tf_op | source)
XLA Modules:
  0.0 634.3 jit_solution(5631509934305473025)
XLA Ops:
  10.3 8.0 %all-to-all-start = ((bf16[8,128,1024]{1,2,0:T(8,128)(2,1)}), bf16[8,128,1024]{1,2,0:T(8,128)(2,1)}, u32[]{:S(2)}, u32[]{:S(2)}) async-start(bf16[8,128,1024]{1,2,0:T(8,128)(2,1)} %tile.10), calls=%async_computation | async-start | bytes 4194304 | tf_op jit(solution)/shard_map/all_to_all | solution.py:53
  25.1 21.3 %all-to-all-done = bf16[8,128,1024]{1,2,0:T(8,128)(2,1)} async-done(((bf16[8,128,1024]{1,2,0:T(8,128)(2,1)}), bf16[8,128,1024]{1,2,0:T(8,128)(2,1)}, u32[]{:S(2)}, u32[]{:S(2)}) %all-to-all-start) | async-done | bytes 2097184 | tf_op jit(solution)/shard_map/all_to_all | solution.py:53
  46.4 2.9 copy.277
  52.8 2.6 fusion.45
  57.1 2.7 collective-permute-start.5
  68.6 4.4 collective-permute-done.7
  73.9 21.8 %shard_map.229 = (bf16[1024,128]{1,0:T(8,128)(2,1)S(1)}, f32[8,64,256]{2,1,0:T(8,128)S(1)}, f32[8,1,256]{2,1,0:T(1,128)S(1)}) custom-call(s32[16]{0:T(128)S(1)} %select_reduce_fusion.2.order_ref, s32[16]{0:T(128)S(1)} %lt.91.qnum_ref, s32[64]{0:T(128)S(1)} %reshape.375.knum_ref, bf16[2,1024,128]{2,1,0:T(8,128)(2,1)S(1)} %pad.8.q_ref, ...), custom_call_target="tpu_custom_call" | custom-call | flops 12000000000 | bytes 4000000 | tf_op jit(solution)/shard_map/pallas_call | solution.py:240
  96.5 5.5 all-to-all-start.1
  103.7 2.3 bitcast_dynamic-update-slice_fusion.4
  106.0 2.3 bitcast_dynamic-update-slice_fusion.5
  108.2 3.2 all-to-all-done.1
  117.8 2.6 convolution_convert_fusion.2
  120.4 5.0 all-to-all-start.2
  127.2 4.0 convolution_convert_fusion
  131.2 35.2 %all-to-all-done.2 = bf16[32,48,1024]{2,1,0:T(8,128)(2,1)} async-done(((bf16[32,48,1024]{2,1,0:T(8,128)(2,1)}), bf16[32,48,1024]{2,1,0:T(8,128)(2,1)}, u32[]{:S(2)}, u32[]{:S(2)}) %all-to-all-start.2) | async-done | bytes 3145760 | tf_op jit(solution)/shard_map/all_to_all | solution.py:53
  166.4 8.5 %all-to-all-start.3 = ((bf16[32,48,1152]{2,1,0:T(8,128)(2,1)}), bf16[32,48,1152]{2,1,0:T(8,128)(2,1)}, u32[]{:S(2)}, u32[]{:S(2)}) async-start(bf16[32,48,1152]{2,1,0:T(8,128)(2,1)} %bitcast.289), calls=%async_computation.3 | async-start | bytes 7077888 | tf_op jit(solution)/shard_map/all_to_all | solution.py:53
  178.8 50.0 %collective-permute-done.11 = bf16[256,1024]{1,0:T(8,128)(2,1)} collective-permute-done((bf16[256,1024]{1,0:T(8,128)(2,1)}, bf16[256,1024]{1,0:T(8,128)(2,1)}, u32[]{:S(2)}, u32[]{:S(2)}) %collective-permute-start.11) | collective-permute-done | bytes 524320 | tf_op jit(solution)/shard_map/ppermute | solution.py:45
  230.0 3.2 collective-permute-done.13
  237.6 7.3 %fusion.104 = f32[1536,1024]{0,1:T(8,128)} fusion(bf16[1536,1024]{1,0:T(8,128)(2,1)} %bitcast.46, bf16[1024,1024]{1,0:T(8,128)(2,1)S(1)} %bitcast.303), kind=kOutput, calls=%fused_computation.255 | convolution fusion | flops 3221225472 | bytes 11534336 | tf_op jit(solution)/shard_map/dot_general | solution.py:33
  246.7 3.9 slice.170
  251.8 2.9 fusion.102
  254.9 4.7 copy.332
  259.6 8.8 %multiply_convert_fusion.2 = (bf16[1536,512]{0,1:T(8,128)(2,1)}, bf16[1536,512]{0,1:T(8,128)(2,1)}, bf16[1536,512]{0,1:T(8,128)(2,1)S(1)}) fusion(f32[1536,1024]{0,1:T(8,128)} %fusion.104, bf16[512,1024]{1,0:T(8,128)(2,1)} %bitcast.315, bf16[1536,1024]{0,1:T(8,128)(2,1)} %copy.332, f32[1536]{0:T(1024)S(1)} %broadcast_multiply_fusion.1), kind=kOutput, calls=%fused_computation.24 | convolution fusion | flops 1627127808 | bytes 15210496 | tf_op jit(solution)/shard_map/dot_general | solution.py:37
  268.4 3.9 fusion.2
  273.0 13.7 %all-to-all-start.5 = ((f32[32,1,48]{2,1,0:T(1,128)}), f32[32,1,48]{2,1,0:T(1,128)S(1)}, u32[]{:S(2)}, u32[]{:S(2)}) async-start(f32[32,1,48]{2,1,0:T(1,128)} %all_to_all.83), calls=%async_computation.5 | async-start | bytes 32768 | tf_op jit(solution)/shard_map/all_to_all | solution.py:53
  286.6 7.8 %convolution_convert_fusion.3 = bf16[1536,1024]{1,0:T(8,128)(2,1)} fusion(bf16[1024,1024]{1,0:T(8,128)(2,1)} %bitcast.304, bf16[1536,512]{0,1:T(8,128)(2,1)} %get-tuple-element.139, bf16[1536,512]{0,1:T(8,128)(2,1)} %get-tuple-element.138), kind=kOutput, calls=%fused_computation.16 | convolution fusion | flops 3229089792 | bytes 8388608 | tf_op jit(solution)/shard_map/dot_general | solution.py:37
  296.9 8.2 %all-to-all-start.4 = ((bf16[32,48,1024]{2,1,0:T(8,128)(2,1)}), bf16[32,48,1024]{2,1,0:T(8,128)(2,1)}, u32[]{:S(2)}, u32[]{:S(2)}) async-start(bf16[32,48,1024]{2,1,0:T(8,128)(2,1)} %bitcast.299), calls=%async_computation.4 | async-start | bytes 6291456 | tf_op jit(solution)/shard_map/all_to_all | solution.py:53
  305.1 3.5 fusion.4
  308.6 4.0 copy.329
  312.6 3.8 pad_maximum_fusion
  317.4 29.0 %all-to-all-done.4 = bf16[32,48,1024]{2,1,0:T(8,128)(2,1)} async-done(((bf16[32,48,1024]{2,1,0:T(8,128)(2,1)}), bf16[32,48,1024]{2,1,0:T(8,128)(2,1)}, u32[]{:S(2)}, u32[]{:S(2)}) %all-to-all-start.4) | async-done | bytes 3145760 | tf_op jit(solution)/shard_map/all_to_all | solution.py:53
  346.4 2.6 convolution_bitcast_fusion.2
  352.5 2.4 convolution_convert_fusion.6
  355.8 5.6 all-to-all-start.7
  363.1 3.1 convolution_convert_fusion.4
  366.9 5.1 concatenate.93
  372.0 2.4 dynamic-slice_bitcast_fusion
  377.9 20.6 %shard_map.230 = (f32[1024,128]{1,0:T(8,128)S(1)}, bf16[1024,128]{1,0:T(8,128)(2,1)S(1)}, bf16[1024,128]{1,0:T(8,128)(2,1)S(1)}, bf16[1024,128]{1,0:T(8,128)(2,1)S(1)}, bf16[1024,128]{1,0:T(8,128)(2,1)S(1)}) custom-call(s32[16]{0:T(128)S(1)} %select_reduce_fusion.2.order_ref, s32[16]{0:T(128)S(1)} %lt.91.qnum_ref, s32[64]{0:T(128)S(1)} %reshape.375.knum_ref, ...), custom_call_target="tpu_custom_call" | custom-call | flops 30000001024 | bytes 6000000 | tf_op jit(solution)/shard_map/pallas_call | solution.py:258
  405.3 4.3 collective-permute-done.15
  409.6 3.1 collective-permute-done.16
  412.7 4.8 collective-permute-done.17
  417.8 2.5 fusion.50
  429.4 4.7 copy.320
  434.1 11.4 %collective-permute-done.21 = bf16[256,256]{1,0:T(8,128)(2,1)S(1)} collective-permute-done((bf16[256,256]{1,0:T(8,128)(2,1)S(1)}, bf16[256,256]{1,0:T(8,128)(2,1)S(1)}, u32[]{:S(2)}, u32[]{:S(2)}) %collective-permute-start.21) | collective-permute-done | bytes 131104 | tf_op jit(solution)/shard_map/ppermute | solution.py:45
  447.4 2.3 collective-permute-start.24
  451.7 9.3 %all-to-all-start.11 = ((bf16[32,8,1152]{2,1,0:T(8,128)(2,1)}), bf16[32,8,1152]{2,1,0:T(8,128)(2,1)S(1)}, u32[]{:S(2)}, u32[]{:S(2)}) async-start(bf16[32,8,1152]{2,1,0:T(8,128)(2,1)} %fusion.33), calls=%async_computation.11 | async-start | bytes 1179648 | tf_op jit(solution)/shard_map/all_to_all | solution.py:53
  461.0 6.3 fusion.12
  469.2 4.5 all-to-all-done.11
  474.9 4.2 all-to-all-start.10
  479.2 4.2 fusion.19
  486.4 9.1 %all-to-all-done.10 = bf16[8,256,256]{1,2,0:T(8,128)(2,1)} async-done(((bf16[8,256,256]{1,2,0:T(8,128)(2,1)}), bf16[8,256,256]{1,2,0:T(8,128)(2,1)}, u32[]{:S(2)}, u32[]{:S(2)}) %all-to-all-start.10) | async-done | bytes 1048608 | tf_op jit(solution)/shard_map/all_to_all | solution.py:53
  496.4 4.4 all-to-all-start.12
  502.7 4.8 copy.306
  513.1 9.8 %all-to-all-done.12 = bf16[32,8,1152]{2,1,0:T(8,128)(2,1)S(1)} async-done(((bf16[32,8,1152]{2,1,0:T(8,128)(2,1)}), bf16[32,8,1152]{2,1,0:T(8,128)(2,1)S(1)}, u32[]{:S(2)}, u32[]{:S(2)}) %all-to-all-start.12) | async-done | bytes 589856 | tf_op jit(solution)/shard_map/all_to_all | solution.py:53
  523.7 4.2 all-to-all-start.6
  529.8 2.6 copy.314
  532.4 2.4 constant_dynamic-update-slice_fusion
  545.5 2.5 copy.322
  552.1 27.1 %collective-permute-done.28 = bf16[384,1024]{1,0:T(8,128)(2,1)} collective-permute-done((bf16[384,1024]{1,0:T(8,128)(2,1)}, bf16[384,1024]{1,0:T(8,128)(2,1)}, u32[]{:S(2)}, u32[]{:S(2)}) %collective-permute-start.28) | collective-permute-done | bytes 786464 | tf_op jit(solution)/shard_map/ppermute | solution.py:45
  588.5 12.2 %all-to-all-start.8 = ((bf16[8,128,256]{1,2,0:T(8,128)(2,1)}), bf16[8,128,256]{1,2,0:T(8,128)(2,1)}, u32[]{:S(2)}, u32[]{:S(2)}) async-start(bf16[8,128,256]{1,2,0:T(8,128)(2,1)} %pad_maximum_fusion.4), calls=%async_computation.8 | async-start | bytes 1048576 | tf_op jit(solution)/shard_map/all_to_all | solution.py:53
  605.8 3.4 copy.334
  610.8 4.0 fusion.43
  615.7 8.0 %all-to-all-start.9 = ((f32[128,1,256]{2,1,0:T(1,128)}), f32[128,1,256]{2,1,0:T(1,128)S(1)}, u32[]{:S(2)}, u32[]{:S(2)}) async-start(f32[128,1,256]{2,1,0:T(1,128)} %all_to_all.89), calls=%async_computation.9 | async-start | bytes 262144 | tf_op jit(solution)/shard_map/all_to_all | solution.py:53
  624.9 8.2 %all-to-all-done.9 = f32[128,1,256]{2,1,0:T(1,128)S(1)} async-done(((f32[128,1,256]{2,1,0:T(1,128)}), f32[128,1,256]{2,1,0:T(1,128)S(1)}, u32[]{:S(2)}, u32[]{:S(2)}) %all-to-all-start.9) | async-done | bytes 131104 | tf_op jit(solution)/shard_map/all_to_all | solution.py:53
  (361 shorter events, 138.8 us)
Async XLA Ops:
  6.2 17.2 %collective-permute-start.2 = (bf16[256,256]{1,0:T(8,128)(2,1)S(1)}, bf16[256,256]{1,0:T(8,128)(2,1)S(1)}, u32[]{:S(2)}, u32[]{:S(2)}) collective-permute-start(bf16[256,256]{1,0:T(8,128)(2,1)S(1)} %bitcast.323), channel_id=1, source_target_pairs={{0,2},{2,0},{1,3},{3,1},{4,6},{6,4},{5,7},{7,5},{8,10},{10,8},{9,1... | collective-permute-start | bytes 393224 | tf_op jit(solution)/shard_map/ppermute | solution.py:45
  8.0 14.1 %collective-permute-start = (bf16[2,256]{1,0:T(2,128)(2,1)S(1)}, bf16[2,256]{1,0:T(2,128)(2,1)S(1)}, u32[]{:S(2)}, u32[]{:S(2)}) collective-permute-start(bf16[2,256]{1,0:T(2,128)(2,1)S(1)} %get-tuple-element.137), channel_id=1, source_target_pairs={{0,2},{2,0},{1,3},{3,1},{4,6},{6,4},{5,7},{7,5},{8,10},{10,8},{9,1... | collective-permute-start | bytes 3080 | tf_op jit(solution)/shard_map/ppermute | solution.py:45
  8.6 9.8 %copy-start.63 = (s32[32]{0:T(128)S(1)}, s32[32]{0:T(128)}, u32[]{:S(2)}) copy-start(s32[32]{0:T(128)} %param.16) | copy-start | bytes 388
  8.7 11.0 %copy-start.59 = (s32[1,128,8]{1,2,0:T(8,128)S(1)}, s32[1,128,8]{1,2,0:T(8,128)}, u32[]{:S(2)}) copy-start(s32[1,128,8]{1,2,0:T(8,128)} %param.15) | copy-start | bytes 12292
  8.7 11.0 %copy-start.41 = (bf16[1,256,512]{2,1,0:T(8,128)(2,1)S(1)}, bf16[1,256,512]{2,1,0:T(8,128)(2,1)}, u32[]{:S(2)}) copy-start(bf16[1,256,512]{2,1,0:T(8,128)(2,1)} %param.25) | copy-start | bytes 786436
  8.7 11.0 %copy-start.42 = (bf16[1,256,512]{2,1,0:T(8,128)(2,1)S(1)}, bf16[1,256,512]{2,1,0:T(8,128)(2,1)}, u32[]{:S(2)}) copy-start(bf16[1,256,512]{2,1,0:T(8,128)(2,1)} %param.24) | copy-start | bytes 786436
  10.3 36.1 %all-to-all-start = ((bf16[8,128,1024]{1,2,0:T(8,128)(2,1)}), bf16[8,128,1024]{1,2,0:T(8,128)(2,1)}, u32[]{:S(2)}, u32[]{:S(2)}) async-start(bf16[8,128,1024]{1,2,0:T(8,128)(2,1)} %tile.10), calls=%async_computation | async-start | bytes 4194304 | tf_op jit(solution)/shard_map/all_to_all | solution.py:53
  22.2 1.2 collective-permute-start.1
  23.5 1.6 collective-permute-start.3
  55.5 18.4 %collective-permute-start.4 = (bf16[1024,128]{1,0:T(8,128)(2,1)S(1)}, bf16[1024,128]{1,0:T(8,128)(2,1)S(1)}, u32[]{:S(2)}, u32[]{:S(2)}) collective-permute-start(bf16[1024,128]{1,0:T(8,128)(2,1)S(1)} %pad_maximum_fusion.5.kv0), channel_id=1, source_target_pairs={{0,32},{32,64},{64,96},{96,0},{1,33},{33,65},{65,97},{97,1},{2,34}... | collective-permute-start | bytes 786440 | tf_op jit(solution)/shard_map/ppermute | solution.py:49
  57.1 16.8 %collective-permute-start.5 = (bf16[1024,128]{1,0:T(8,128)(2,1)S(1)}, bf16[1024,128]{1,0:T(8,128)(2,1)S(1)}, u32[]{:S(2)}, u32[]{:S(2)}) collective-permute-start(bf16[1024,128]{1,0:T(8,128)(2,1)S(1)} %pad_maximum_fusion.5.kv0), channel_id=1, source_target_pairs={{0,64},{32,96},{64,0},{96,32},{1,65},{33,97},{65,1},{97,33},{2,66}... | collective-permute-start | bytes 786440 | tf_op jit(solution)/shard_map/ppermute | solution.py:49
  59.8 14.1 %collective-permute-start.6 = (bf16[1024,128]{1,0:T(8,128)(2,1)S(1)}, bf16[1024,128]{1,0:T(8,128)(2,1)S(1)}, u32[]{:S(2)}, u32[]{:S(2)}) collective-permute-start(bf16[1024,128]{1,0:T(8,128)(2,1)S(1)} %pad_maximum_fusion.5.kv0), channel_id=1, source_target_pairs={{0,96},{32,0},{64,32},{96,64},{1,97},{33,1},{65,33},{97,65},{2,98}... | collective-permute-start | bytes 786440 | tf_op jit(solution)/shard_map/ppermute | solution.py:49
  61.3 5.0 collective-permute-start.9
  61.9 11.1 %collective-permute-start.7 = (bf16[256,1024]{1,0:T(8,128)(2,1)}, bf16[256,1024]{1,0:T(8,128)(2,1)S(1)}, u32[]{:S(2)}, u32[]{:S(2)}) collective-permute-start(bf16[256,1024]{1,0:T(8,128)(2,1)} %param.21), channel_id=1, source_target_pairs={{0,2},{2,0},{1,3},{3,1},{4,6},{6,4},{5,7},{7,5},{8,10},{10,8},{9,1... | collective-permute-start | bytes 1572872 | tf_op jit(solution)/shard_map/ppermute | solution.py:45
  66.3 1.3 collective-permute-start.10
  68.6 46.6 %copy-start.27 = (bf16[1024,32]{0,1:T(8,128)(2,1)}, bf16[1024,32]{0,1:T(8,128)(2,1)S(1)}, u32[]{:S(2)}) copy-start(bf16[1024,32]{0,1:T(8,128)(2,1)S(1)} %reshape_reshape.20) | copy-start | bytes 196612
  73.9 32.1 %collective-permute-start.8 = (bf16[2,256,1024]{2,1,0:T(8,128)(2,1)}, bf16[2,256,1024]{2,1,0:T(8,128)(2,1)}, u32[]{:S(2)}, u32[]{:S(2)}) collective-permute-start(bf16[2,256,1024]{2,1,0:T(8,128)(2,1)} %bitcast_dynamic-update-slice_fusion.10), channel_id=1, source_target_pairs={{0,1},{1,0},{2,3},{3,2},{4,5},{5,4},{6,7},{7,6},{8,9},{9,8},{10,11... | collective-permute-start | bytes 3145736 | tf_op jit(solution)/shard_map/ppermute | solution.py:45
  96.5 14.9 %all-to-all-start.1 = ((bf16[8,128,128]{1,2,0:T(8,128)(2,1)}), bf16[8,128,128]{1,2,0:T(8,128)(2,1)S(1)}, u32[]{:S(2)}, u32[]{:S(2)}) async-start(bf16[8,128,128]{1,2,0:T(8,128)(2,1)} %copy.295), calls=%async_computation.1 | async-start | bytes 524288 | tf_op jit(solution)/shard_map/all_to_all | solution.py:53
  105.9 10.6 %copy-start.66 = (s32[128]{0:T(128)S(1)}, s32[128]{0:T(128)}, u32[]{:S(2)}) copy-start(s32[128]{0:T(128)} %iota_add_fusion) | copy-start | bytes 1540
  114.4 235.7 %copy-start.1 = (f32[128,1024]{1,0:T(8,128)}, f32[128,1024]{1,0:T(8,128)S(1)}, u32[]{:S(2)}) copy-start(f32[128,1024]{1,0:T(8,128)S(1)} %get-tuple-element.170) | copy-start | bytes 1572868
  120.4 46.0 %all-to-all-start.2 = ((bf16[32,48,1024]{2,1,0:T(8,128)(2,1)}), bf16[32,48,1024]{2,1,0:T(8,128)(2,1)}, u32[]{:S(2)}, u32[]{:S(2)}) async-start(bf16[32,48,1024]{2,1,0:T(8,128)(2,1)} %bitcast.291), calls=%async_computation.2 | async-start | bytes 6291456 | tf_op jit(solution)/shard_map/all_to_all | solution.py:53
  166.4 78.5 %all-to-all-start.3 = ((bf16[32,48,1152]{2,1,0:T(8,128)(2,1)}), bf16[32,48,1152]{2,1,0:T(8,128)(2,1)}, u32[]{:S(2)}, u32[]{:S(2)}) async-start(bf16[32,48,1152]{2,1,0:T(8,128)(2,1)} %bitcast.289), calls=%async_computation.3 | async-start | bytes 7077888 | tf_op jit(solution)/shard_map/all_to_all | solution.py:53
  174.9 53.8 %collective-permute-start.11 = (bf16[256,1024]{1,0:T(8,128)(2,1)}, bf16[256,1024]{1,0:T(8,128)(2,1)}, u32[]{:S(2)}, u32[]{:S(2)}) collective-permute-start(bf16[256,1024]{1,0:T(8,128)(2,1)} %pad_maximum_fusion.3), channel_id=1, source_target_pairs={{0,2},{2,0},{1,3},{3,1},{4,6},{6,4},{5,7},{7,5},{8,10},{10,8},{9,1... | collective-permute-start | bytes 1572872 | tf_op jit(solution)/shard_map/ppermute | solution.py:45
  176.1 53.9 %copy-start.40 = (bf16[1,128,1024]{2,1,0:T(8,128)(2,1)S(1)}, bf16[1,128,1024]{2,1,0:T(8,128)(2,1)}, u32[]{:S(2)}) copy-start(bf16[1,128,1024]{2,1,0:T(8,128)(2,1)} %param.26) | copy-start | bytes 786436
  176.6 56.6 %collective-permute-start.13 = (bf16[128,1024]{1,0:T(8,128)(2,1)}, bf16[128,1024]{1,0:T(8,128)(2,1)S(1)}, u32[]{:S(2)}, u32[]{:S(2)}) collective-permute-start(bf16[128,1024]{1,0:T(8,128)(2,1)} %bitcast.324), channel_id=1, source_target_pairs={{0,2},{2,0},{1,3},{3,1},{4,6},{6,4},{5,7},{7,5},{8,10},{10,8},{9,1... | collective-permute-start | bytes 786440 | tf_op jit(solution)/shard_map/ppermute | solution.py:45
  229.8 5.5 collective-permute-start.12
  233.2 2.0 collective-permute-start.14
  273.0 23.3 %all-to-all-start.5 = ((f32[32,1,48]{2,1,0:T(1,128)}), f32[32,1,48]{2,1,0:T(1,128)S(1)}, u32[]{:S(2)}, u32[]{:S(2)}) async-start(f32[32,1,48]{2,1,0:T(1,128)} %all_to_all.83), calls=%async_computation.5 | async-start | bytes 32768 | tf_op jit(solution)/shard_map/all_to_all | solution.py:53
  296.9 49.5 %all-to-all-start.4 = ((bf16[32,48,1024]{2,1,0:T(8,128)(2,1)}), bf16[32,48,1024]{2,1,0:T(8,128)(2,1)}, u32[]{:S(2)}, u32[]{:S(2)}) async-start(bf16[32,48,1024]{2,1,0:T(8,128)(2,1)} %bitcast.299), calls=%async_computation.4 | async-start | bytes 6291456 | tf_op jit(solution)/shard_map/all_to_all | solution.py:53
  316.4 32.6 %copy-start.28 = (bf16[1024,32]{0,1:T(8,128)(2,1)S(1)}, bf16[1024,32]{0,1:T(8,128)(2,1)}, u32[]{:S(2)}) copy-start(bf16[1024,32]{0,1:T(8,128)(2,1)} %copy-done.27) | copy-start | bytes 196612
  317.4 31.6 %copy-start.45 = (bf16[128,32]{0,1:T(8,128)(2,1)S(1)}, bf16[128,32]{0,1:T(8,128)(2,1)}, u32[]{:S(2)}) copy-start(bf16[128,32]{0,1:T(8,128)(2,1)} %fusion.79) | copy-start | bytes 24580
  350.1 16.1 %copy-start.60 = (f32[128]{0:T(128)}, f32[128]{0:T(128)S(1)}, u32[]{:S(2)}) copy-start(f32[128]{0:T(128)S(1)} %broadcast_multiply_fusion.3) | copy-start | bytes 1540
  355.8 18.8 %all-to-all-start.7 = ((bf16[8,128,128]{1,2,0:T(8,128)(2,1)}), bf16[8,128,128]{1,2,0:T(8,128)(2,1)}, u32[]{:S(2)}, u32[]{:S(2)}) async-start(bf16[8,128,128]{1,2,0:T(8,128)(2,1)} %bitcast.68), calls=%async_computation.7 | async-start | bytes 524288 | tf_op jit(solution)/shard_map/all_to_all | solution.py:53
  374.4 49.7 %collective-permute-start.25 = (bf16[2,256,1152]{2,1,0:T(8,128)(2,1)}, bf16[2,256,1152]{2,1,0:T(8,128)(2,1)}, u32[]{:S(2)}, u32[]{:S(2)}) collective-permute-start(bf16[2,256,1152]{2,1,0:T(8,128)(2,1)} %dynamic-slice_bitcast_fusion), channel_id=1, source_target_pairs={{0,1},{1,0},{2,3},{3,2},{4,5},{5,4},{6,7},{7,6},{8,9},{9,8},{10,11... | collective-permute-start | bytes 3538952 | tf_op jit(solution)/shard_map/ppermute | solution.py:45
  400.4 9.2 %collective-permute-start.15 = (bf16[1024,128]{1,0:T(8,128)(2,1)S(1)}, bf16[1024,128]{1,0:T(8,128)(2,1)S(1)}, u32[]{:S(2)}, u32[]{:S(2)}) collective-permute-start(bf16[1024,128]{1,0:T(8,128)(2,1)S(1)} %get-tuple-element.47), channel_id=1, source_target_pairs={{0,96},{32,0},{64,32},{96,64},{1,97},{33,1},{65,33},{97,65},{2,98}... | collective-permute-start | bytes 786440 | tf_op jit(solution)/shard_map/ppermute | solution.py:49
  402.0 10.7 %collective-permute-start.16 = (bf16[1024,128]{1,0:T(8,128)(2,1)S(1)}, bf16[1024,128]{1,0:T(8,128)(2,1)S(1)}, u32[]{:S(2)}, u32[]{:S(2)}) collective-permute-start(bf16[1024,128]{1,0:T(8,128)(2,1)S(1)} %get-tuple-element.48), channel_id=1, source_target_pairs={{0,64},{32,96},{64,0},{96,32},{1,65},{33,97},{65,1},{97,33},{2,66}... | collective-permute-start | bytes 786440 | tf_op jit(solution)/shard_map/ppermute | solution.py:49
  404.0 13.5 %collective-permute-start.17 = (bf16[1024,128]{1,0:T(8,128)(2,1)S(1)}, bf16[1024,128]{1,0:T(8,128)(2,1)S(1)}, u32[]{:S(2)}, u32[]{:S(2)}) collective-permute-start(bf16[1024,128]{1,0:T(8,128)(2,1)S(1)} %get-tuple-element.49), channel_id=1, source_target_pairs={{0,32},{32,64},{64,96},{96,0},{1,33},{33,65},{65,97},{97,1},{2,34}... | collective-permute-start | bytes 786440 | tf_op jit(solution)/shard_map/ppermute | solution.py:49
  423.9 3.5 collective-permute-start.20
  427.2 22.5 %collective-permute-start.26 = (bf16[256,1152]{1,0:T(8,128)(2,1)}, bf16[256,1152]{1,0:T(8,128)(2,1)}, u32[]{:S(2)}, u32[]{:S(2)}) collective-permute-start(bf16[256,1152]{1,0:T(8,128)(2,1)} %fusion.32), channel_id=1, source_target_pairs={{0,2},{2,0},{1,3},{3,1},{4,6},{6,4},{5,7},{7,5},{8,10},{10,8},{9,1... | collective-permute-start | bytes 1769480 | tf_op jit(solution)/shard_map/ppermute | solution.py:45
  427.5 18.0 %collective-permute-start.21 = (bf16[256,256]{1,0:T(8,128)(2,1)S(1)}, bf16[256,256]{1,0:T(8,128)(2,1)S(1)}, u32[]{:S(2)}, u32[]{:S(2)}) collective-permute-start(bf16[256,256]{1,0:T(8,128)(2,1)S(1)} %fusion.73), channel_id=1, source_target_pairs={{0,2},{2,0},{1,3},{3,1},{4,6},{6,4},{5,7},{7,5},{8,10},{10,8},{9,1... | collective-permute-start | bytes 393224 | tf_op jit(solution)/shard_map/ppermute | solution.py:45
  445.5 21.8 %collective-permute-start.22 = (bf16[256,256]{1,0:T(8,128)(2,1)S(1)}, bf16[256,256]{1,0:T(8,128)(2,1)S(1)}, u32[]{:S(2)}, u32[]{:S(2)}) collective-permute-start(bf16[256,256]{1,0:T(8,128)(2,1)S(1)} %fusion.71), channel_id=1, source_target_pairs={{0,32},{32,64},{64,96},{96,0},{1,33},{33,65},{65,97},{97,1},{2,34}... | collective-permute-start | bytes 393224 | tf_op jit(solution)/shard_map/ppermute | solution.py:49
  445.9 21.4 %collective-permute-start.23 = (bf16[256,256]{1,0:T(8,128)(2,1)S(1)}, bf16[256,256]{1,0:T(8,128)(2,1)S(1)}, u32[]{:S(2)}, u32[]{:S(2)}) collective-permute-start(bf16[256,256]{1,0:T(8,128)(2,1)S(1)} %fusion.71), channel_id=1, source_target_pairs={{0,64},{32,96},{64,0},{96,32},{1,65},{33,97},{65,1},{97,33},{2,66}... | collective-permute-start | bytes 393224 | tf_op jit(solution)/shard_map/ppermute | solution.py:49
  447.4 20.6 %collective-permute-start.24 = (bf16[256,256]{1,0:T(8,128)(2,1)S(1)}, bf16[256,256]{1,0:T(8,128)(2,1)}, u32[]{:S(2)}, u32[]{:S(2)}) collective-permute-start(bf16[256,256]{1,0:T(8,128)(2,1)S(1)} %fusion.71), channel_id=1, source_target_pairs={{0,96},{32,0},{64,32},{96,64},{1,97},{33,1},{65,33},{97,65},{2,98}... | collective-permute-start | bytes 393224 | tf_op jit(solution)/shard_map/ppermute | solution.py:49
  451.7 22.1 %all-to-all-start.11 = ((bf16[32,8,1152]{2,1,0:T(8,128)(2,1)}), bf16[32,8,1152]{2,1,0:T(8,128)(2,1)S(1)}, u32[]{:S(2)}, u32[]{:S(2)}) async-start(bf16[32,8,1152]{2,1,0:T(8,128)(2,1)} %fusion.33), calls=%async_computation.11 | async-start | bytes 1179648 | tf_op jit(solution)/shard_map/all_to_all | solution.py:53
  467.3 16.1 %copy-start.8 = (bf16[2,2,256,1024]{3,2,1,0:T(8,128)(2,1)}, bf16[2,2,256,1024]{3,2,1,0:T(8,128)(2,1)S(1)}, u32[]{:S(2)}) copy-start(bf16[2,2,256,1024]{3,2,1,0:T(8,128)(2,1)S(1)} %fusion.12) | copy-start | bytes 6291460
  467.3 11.9 %copy-start.54 = (f32[1536]{0:T(1024)S(1)}, f32[1536]{0:T(1024)}, u32[]{:S(2)}) copy-start(f32[1536]{0:T(1024)} %copy-done.53) | copy-start | bytes 18436
  474.9 20.6 %all-to-all-start.10 = ((bf16[8,256,256]{1,2,0:T(8,128)(2,1)}), bf16[8,256,256]{1,2,0:T(8,128)(2,1)}, u32[]{:S(2)}, u32[]{:S(2)}) async-start(bf16[8,256,256]{1,2,0:T(8,128)(2,1)} %tile.13), calls=%async_computation.10 | async-start | bytes 2097152 | tf_op jit(solution)/shard_map/all_to_all | solution.py:53
  483.4 13.0 %copy-start.14 = (bf16[512,1024]{1,0:T(8,128)(2,1)}, bf16[512,1024]{1,0:T(8,128)(2,1)S(1)}, u32[]{:S(2)}) copy-start(bf16[512,1024]{1,0:T(8,128)(2,1)S(1)} %fusion.19) | copy-start | bytes 3145732
  483.4 17.4 %copy-start.52 = (f32[128]{0:T(128)S(1)}, f32[128]{0:T(128)}, u32[]{:S(2)}) copy-start(f32[128]{0:T(128)} %get-tuple-element.134) | copy-start | bytes 1540
  483.4 17.4 %copy-start.58 = (f32[128]{0:T(128)S(1)}, f32[128]{0:T(128)}, u32[]{:S(2)}) copy-start(f32[128]{0:T(128)} %copy-done.57) | copy-start | bytes 1540
  484.9 50.0 %collective-permute-start.27 = (bf16[2,384,1024]{2,1,0:T(8,128)(2,1)}, bf16[2,384,1024]{2,1,0:T(8,128)(2,1)}, u32[]{:S(2)}, u32[]{:S(2)}) collective-permute-start(bf16[2,384,1024]{2,1,0:T(8,128)(2,1)} %fusion.16), channel_id=1, source_target_pairs={{0,1},{1,0},{2,3},{3,2},{4,5},{5,4},{6,7},{7,6},{8,9},{9,8},{10,11... | collective-permute-start | bytes 4718600 | tf_op jit(solution)/shard_map/ppermute | solution.py:45
  484.9 44.9 %collective-permute-start.18 = (bf16[256,8,256]{0,2,1:T(8,128)(2,1)}, bf16[256,8,256]{0,2,1:T(8,128)(2,1)}, u32[]{:S(2)}, u32[]{:S(2)}) collective-permute-start(bf16[256,8,256]{0,2,1:T(8,128)(2,1)} %pad_maximum_fusion.1), channel_id=1, source_target_pairs={{0,2},{2,0},{1,3},{3,1},{4,6},{6,4},{5,7},{7,5},{8,10},{10,8},{9,1... | collective-permute-start | bytes 3145736 | tf_op jit(solution)/shard_map/ppermute | solution.py:45
  496.4 26.5 %all-to-all-start.12 = ((bf16[32,8,1152]{2,1,0:T(8,128)(2,1)}), bf16[32,8,1152]{2,1,0:T(8,128)(2,1)S(1)}, u32[]{:S(2)}, u32[]{:S(2)}) async-start(bf16[32,8,1152]{2,1,0:T(8,128)(2,1)} %tile.14), calls=%async_computation.12 | async-start | bytes 1179648 | tf_op jit(solution)/shard_map/all_to_all | solution.py:53
  523.7 64.8 %all-to-all-start.6 = ((bf16[32,48,1024]{2,1,0:T(8,128)(2,1)}), bf16[32,48,1024]{2,1,0:T(8,128)(2,1)S(1)}, u32[]{:S(2)}, u32[]{:S(2)}) async-start(bf16[32,48,1024]{2,1,0:T(8,128)(2,1)} %bitcast.290), calls=%async_computation.6 | async-start | bytes 6291456 | tf_op jit(solution)/shard_map/all_to_all | solution.py:53
  534.9 68.2 %collective-permute-start.19 = (bf16[2,256,8,256]{3,2,1,0:T(8,128)(2,1)}, bf16[2,256,8,256]{3,2,1,0:T(8,128)(2,1)}, u32[]{:S(2)}, u32[]{:S(2)}) collective-permute-start(bf16[2,256,8,256]{3,2,1,0:T(8,128)(2,1)} %constant_dynamic-update-slice_fusion), channel_id=1, source_target_pairs={{0,1},{1,0},{2,3},{3,2},{4,5},{5,4},{6,7},{7,6},{8,9},{9,8},{10,11... | collective-permute-start | bytes 6291464 | tf_op jit(solution)/shard_map/ppermute | solution.py:45
  538.8 40.4 %collective-permute-start.28 = (bf16[384,1024]{1,0:T(8,128)(2,1)}, bf16[384,1024]{1,0:T(8,128)(2,1)}, u32[]{:S(2)}, u32[]{:S(2)}) collective-permute-start(bf16[384,1024]{1,0:T(8,128)(2,1)} %fusion.31), channel_id=1, source_target_pairs={{0,2},{2,0},{1,3},{3,1},{4,6},{6,4},{5,7},{7,5},{8,10},{10,8},{9,1... | collective-permute-start | bytes 2359304 | tf_op jit(solution)/shard_map/ppermute | solution.py:45
  552.1 30.9 %copy-start.18 = (bf16[32,8,1152]{2,1,0:T(8,128)(2,1)S(1)}, bf16[32,8,1152]{2,1,0:T(8,128)(2,1)}, u32[]{:S(2)}) copy-start(bf16[32,8,1152]{2,1,0:T(8,128)(2,1)} %copy-done.17) | copy-start | bytes 1769476
  588.5 22.4 %all-to-all-start.8 = ((bf16[8,128,256]{1,2,0:T(8,128)(2,1)}), bf16[8,128,256]{1,2,0:T(8,128)(2,1)}, u32[]{:S(2)}, u32[]{:S(2)}) async-start(bf16[8,128,256]{1,2,0:T(8,128)(2,1)} %pad_maximum_fusion.4), calls=%async_computation.8 | async-start | bytes 1048576 | tf_op jit(solution)/shard_map/all_to_all | solution.py:53
  609.2 14.4 %copy-start.3 = (f32[128,1024]{1,0:T(8,128)S(1)}, f32[128,1024]{1,0:T(8,128)}, u32[]{:S(2)}) copy-start(f32[128,1024]{1,0:T(8,128)} %copy-done.1) | copy-start | bytes 1572868
  609.3 14.5 %copy-start.13 = (f32[128,1024]{1,0:T(8,128)S(1)}, f32[128,1024]{1,0:T(8,128)}, u32[]{:S(2)}) copy-start(f32[128,1024]{1,0:T(8,128)} %copy-done.12) | copy-start | bytes 1572868
  609.3 14.5 %copy-start.22 = (bf16[1,128,1024]{2,1,0:T(8,128)(2,1)S(1)}, bf16[1,128,1024]{2,1,0:T(8,128)(2,1)}, u32[]{:S(2)}) copy-start(bf16[1,128,1024]{2,1,0:T(8,128)(2,1)} %param.27) | copy-start | bytes 786436
  609.3 14.5 %copy-start.56 = (f32[128]{0:T(128)S(1)}, f32[128]{0:T(128)}, u32[]{:S(2)}) copy-start(f32[128]{0:T(128)} %copy-done.55) | copy-start | bytes 1540
  609.3 14.5 %copy-start.61 = (f32[128]{0:T(128)S(1)}, f32[128]{0:T(128)}, u32[]{:S(2)}) copy-start(f32[128]{0:T(128)} %copy-done.60) | copy-start | bytes 1540
  615.7 17.4 %all-to-all-start.9 = ((f32[128,1,256]{2,1,0:T(1,128)}), f32[128,1,256]{2,1,0:T(1,128)S(1)}, u32[]{:S(2)}, u32[]{:S(2)}) async-start(f32[128,1,256]{2,1,0:T(1,128)} %all_to_all.89), calls=%async_computation.9 | async-start | bytes 262144 | tf_op jit(solution)/shard_map/all_to_all | solution.py:53
  (46 other events, 156.6 us)
